TPU v7x, 512 devices: a whole 4x8x8 slice. The times are simulated.
512 devices in a mesh: wide: 64 (over x, z, core), narrow: 8 (over y).
Axes of the slice: x: 4, y: 8, z: 8, core: 2. Of those that a mesh axis runs over, the one named last changes fastest.
Arguments:
- core: float32 [512, 384, 384], P(('wide', 'narrow')), may hold values from -0.25371838 to 0.25371838
- next_core: float32 [384, 512, 384], P(None, ('wide', 'narrow')), may hold values from -37.5 to 37.5
- start_block: float32 [384, 192], replicated, may hold values from -6 to 6
Outputs:
- core_out: float32 [512, 384, 192], P(('wide', 'narrow'))
- next_out: float32 [192, 512, 384], P(None, ('wide', 'narrow'))
All inputs are finite; a program needn't handle non-finite values.
Results may differ from a plain program's by a relative error of at most 0.0003.
Values sent between devices are 32-bit elements; how exact they have to be, the bound alone decides.
A program may use at most 64 MiB of HBM per device.

v0:
```python
import math

import jax
import jax.numpy as jnp
from jax import lax
from jax.sharding import PartitionSpec as P

ITERS = 6


def orthonormal(block):
    square = jnp.dot(
        block.T, block, precision=lax.Precision.HIGHEST, preferred_element_type=jnp.float32
    )
    factor = jnp.linalg.cholesky(square)
    return jax.scipy.linalg.solve_triangular(factor, block.T, lower=True).T


def reduce_all(summands):
    return lax.psum((summands[0],), ("wide", "narrow"))


def shards(core, next_core, start_block):
    highest = lax.Precision.HIGHEST
    mode_dev = core.shape[0]
    core_rank = core.shape[1]
    trunc_rank = start_block.shape[1]
    flat_core = core.reshape(mode_dev * core_rank, core_rank)
    flat_next = next_core.reshape(core_rank, mode_dev * core_rank)
    gram_local = jnp.dot(
        flat_core.T, flat_core, precision=highest, preferred_element_type=jnp.float32
    )
    cross_local = jnp.dot(
        flat_next, flat_next.T, precision=highest, preferred_element_type=jnp.float32
    )
    (gram,) = reduce_all((gram_local,))
    lower_factor = jnp.linalg.cholesky(gram)
    upper_factor = lower_factor.T
    bond_local = jnp.dot(
        jnp.dot(upper_factor, cross_local, precision=highest, preferred_element_type=jnp.float32),
        lower_factor,
        precision=highest,
        preferred_element_type=jnp.float32,
    )
    (bond_gram,) = reduce_all((bond_local,))
    ortho_t = jax.scipy.linalg.solve_triangular(lower_factor, flat_core.T, lower=True)
    moved = jnp.dot(upper_factor, flat_next, precision=highest, preferred_element_type=jnp.float32)
    basis = start_block
    for step in range(ITERS):
        basis = orthonormal(
            jnp.dot(bond_gram, basis, precision=highest, preferred_element_type=jnp.float32)
        )
    total_rows = mode_dev * lax.axis_size("wide") * lax.axis_size("narrow") * core_rank
    scale = math.sqrt(total_rows)
    core_out = scale * jnp.dot(
        ortho_t.T, basis, precision=highest, preferred_element_type=jnp.float32
    )
    next_out = jnp.dot(basis.T, moved, precision=highest, preferred_element_type=jnp.float32)
    return (
        core_out.reshape(mode_dev, core_rank, trunc_rank),
        next_out.reshape(trunc_rank, mode_dev, core_rank),
    )


def solution(mesh):
    placed = (P(("wide", "narrow"), None, None), P(None, ("wide", "narrow"), None), P())
    return jax.shard_map(
        shards,
        mesh=mesh,
        in_specs=placed,
        out_specs=(P(("wide", "narrow"), None, None), P(None, ("wide", "narrow"), None)),
        check_vma=False,
    )
```

profile of v0, /device:TPU:1, one launch (start us, length us, event | category | flops | bytes accessed | tf_op | source)
XLA Modules:
  0.0 950.2 jit_solution(7478780903963215806)
XLA Ops:
  13.0 275.8 %all-reduce.7.cloned.1.call-done = f32[384,384]{0,1:T(8,128)} async-done(((f32[384,384]{0,1:T(8,128)}), f32[384,384]{0,1:T(8,128)}) %all-reduce.7.cloned.1.call-update) | async-done | bytes 589840 | tf_op jit(solution)/shard_map/psum | solution.py:20
  290.2 11.7 %cholesky.122 = f32[128,128]{1,0:T(8,128)S(1)} custom-call(f32[128,128]{1,0:T(8,128)S(1)} %cholesky.736), custom_call_target="Cholesky" | custom-call | tf_op jit(solution)/shard_map/jit(cholesky)/cholesky | solution.py:37
  302.0 9.8 %custom-call.34 = f32[1,128,128]{1,2,0:T(8,128)S(1)} custom-call(f32[1,128,128]{2,1,0:T(8,128)S(1)} %get-tuple-element.92), custom_call_target="InvertDiagBlocksLowerTriangular" | custom-call | tf_op jit(solution)/shard_map/jit(cholesky)/cholesky | solution.py:37
  312.4 11.7 %cholesky.248 = f32[128,128]{1,0:T(8,128)S(1)} custom-call(f32[128,128]{1,0:T(8,128)S(1)} %cholesky.740), custom_call_target="Cholesky" | custom-call | tf_op jit(solution)/shard_map/jit(cholesky)/cholesky | solution.py:37
  324.1 10.3 %custom-call.35 = f32[1,128,128]{1,2,0:T(8,128)S(1)} custom-call(f32[1,128,128]{2,1,0:T(8,128)S(1)} %get-tuple-element.89), custom_call_target="InvertDiagBlocksLowerTriangular" | custom-call | tf_op jit(solution)/shard_map/jit(cholesky)/cholesky | solution.py:37
  334.9 11.7 %cholesky.267 = f32[128,128]{1,0:T(8,128)S(1)} custom-call(f32[128,128]{1,0:T(8,128)S(1)} %convolution_subtract_fusion.9), custom_call_target="Cholesky" | custom-call | tf_op jit(solution)/shard_map/jit(cholesky)/cholesky | solution.py:37
  361.3 30.5 %custom-call.36 = f32[3,128,128]{1,2,0:T(8,128)S(1)} custom-call(f32[3,128,128]{2,1,0:T(8,128)} %get-tuple-element.19), custom_call_target="InvertDiagBlocksLowerTriangular" | custom-call | tf_op jit(solution)/shard_map/jit(_solve_triangular)/triangular_solve | solution.py:46
  395.6 225.0 %all-reduce.9.cloned.1.call-done = f32[384,384]{1,0:T(8,128)} async-done(((f32[384,384]{1,0:T(8,128)}), f32[384,384]{1,0:T(8,128)}) %all-reduce.9.cloned.1.call-update) | async-done | bytes 589840 | tf_op jit(solution)/shard_map/psum | solution.py:20
  623.1 11.7 %cholesky.512 = f32[128,128]{1,0:T(8,128)S(1)} custom-call(f32[128,128]{1,0:T(8,128)S(1)} %cholesky.744), custom_call_target="Cholesky" | custom-call | tf_op jit(solution)/shard_map/jit(cholesky)/cholesky | solution.py:15
  634.9 9.8 %custom-call.47 = f32[1,128,128]{1,2,0:T(8,128)S(1)} custom-call(f32[1,128,128]{2,1,0:T(8,128)S(1)} %get-tuple-element.85), custom_call_target="InvertDiagBlocksLowerTriangular" | custom-call | tf_op jit(solution)/shard_map/jit(cholesky)/cholesky | solution.py:15
  653.8 19.7 %custom-call.48 = f32[2,128,128]{1,2,0:T(8,128)S(1)} custom-call(f32[2,128,128]{2,1,0:T(8,128)S(1)} %pad_maximum_fusion.3), custom_call_target="InvertDiagBlocksLowerTriangular" | custom-call | tf_op jit(solution)/shard_map/jit(_solve_triangular)/triangular_solve | solution.py:16
  675.9 11.7 %cholesky.550 = f32[128,128]{1,0:T(8,128)S(1)} custom-call(f32[128,128]{1,0:T(8,128)S(1)} %cholesky.747), custom_call_target="Cholesky" | custom-call | tf_op jit(solution)/shard_map/jit(cholesky)/cholesky | solution.py:15
  687.7 9.8 %custom-call.49 = f32[1,128,128]{1,2,0:T(8,128)S(1)} custom-call(f32[1,128,128]{2,1,0:T(8,128)S(1)} %get-tuple-element.83), custom_call_target="InvertDiagBlocksLowerTriangular" | custom-call | tf_op jit(solution)/shard_map/jit(cholesky)/cholesky | solution.py:15
  706.7 20.1 %custom-call.50 = f32[2,128,128]{1,2,0:T(8,128)S(1)} custom-call(f32[2,128,128]{2,1,0:T(8,128)S(1)} %pad_maximum_fusion.4), custom_call_target="InvertDiagBlocksLowerTriangular" | custom-call | tf_op jit(solution)/shard_map/jit(_solve_triangular)/triangular_solve | solution.py:16
  729.2 11.7 %cholesky.588 = f32[128,128]{1,0:T(8,128)S(1)} custom-call(f32[128,128]{1,0:T(8,128)S(1)} %cholesky.750), custom_call_target="Cholesky" | custom-call | tf_op jit(solution)/shard_map/jit(cholesky)/cholesky | solution.py:15
  740.9 9.8 %custom-call.51 = f32[1,128,128]{1,2,0:T(8,128)S(1)} custom-call(f32[1,128,128]{2,1,0:T(8,128)S(1)} %get-tuple-element.81), custom_call_target="InvertDiagBlocksLowerTriangular" | custom-call | tf_op jit(solution)/shard_map/jit(cholesky)/cholesky | solution.py:15
  759.9 19.8 %custom-call.52 = f32[2,128,128]{1,2,0:T(8,128)S(1)} custom-call(f32[2,128,128]{2,1,0:T(8,128)S(1)} %pad_maximum_fusion.5), custom_call_target="InvertDiagBlocksLowerTriangular" | custom-call | tf_op jit(solution)/shard_map/jit(_solve_triangular)/triangular_solve | solution.py:16
  782.1 11.7 %cholesky.626 = f32[128,128]{1,0:T(8,128)S(1)} custom-call(f32[128,128]{1,0:T(8,128)S(1)} %cholesky.753), custom_call_target="Cholesky" | custom-call | tf_op jit(solution)/shard_map/jit(cholesky)/cholesky | solution.py:15
  812.9 19.9 %custom-call.54 = f32[2,128,128]{1,2,0:T(8,128)S(1)} custom-call(f32[2,128,128]{2,1,0:T(8,128)S(1)} %pad_maximum_fusion.6), custom_call_target="InvertDiagBlocksLowerTriangular" | custom-call | tf_op jit(solution)/shard_map/jit(_solve_triangular)/triangular_solve | solution.py:16
  835.2 11.7 %cholesky.664 = f32[128,128]{1,0:T(8,128)S(1)} custom-call(f32[128,128]{1,0:T(8,128)S(1)} %cholesky.756), custom_call_target="Cholesky" | custom-call | tf_op jit(solution)/shard_map/jit(cholesky)/cholesky | solution.py:15
  846.9 9.8 %custom-call.55 = f32[1,128,128]{1,2,0:T(8,128)S(1)} custom-call(f32[1,128,128]{2,1,0:T(8,128)S(1)} %get-tuple-element.77), custom_call_target="InvertDiagBlocksLowerTriangular" | custom-call | tf_op jit(solution)/shard_map/jit(cholesky)/cholesky | solution.py:15
  865.9 20.1 %custom-call.56 = f32[2,128,128]{1,2,0:T(8,128)S(1)} custom-call(f32[2,128,128]{2,1,0:T(8,128)S(1)} %pad_maximum_fusion.7), custom_call_target="InvertDiagBlocksLowerTriangular" | custom-call | tf_op jit(solution)/shard_map/jit(_solve_triangular)/triangular_solve | solution.py:16
  888.4 11.7 %cholesky.702 = f32[128,128]{1,0:T(8,128)S(1)} custom-call(f32[128,128]{1,0:T(8,128)S(1)} %cholesky.759), custom_call_target="Cholesky" | custom-call | tf_op jit(solution)/shard_map/jit(cholesky)/cholesky | solution.py:15
  919.1 19.8 %custom-call.58 = f32[2,128,128]{1,2,0:T(8,128)S(1)} custom-call(f32[2,128,128]{2,1,0:T(8,128)S(1)} %pad_maximum_fusion.8), custom_call_target="InvertDiagBlocksLowerTriangular" | custom-call | tf_op jit(solution)/shard_map/jit(_solve_triangular)/triangular_solve | solution.py:16
  (189 shorter events, 117.5 us)
Async XLA Ops:
  7.2 613.4 %copy-start = (f32[384,192]{0,1:T(8,128)S(1)}, f32[384,192]{0,1:T(8,128)}, u32[]{:S(2)}) copy-start(f32[384,192]{0,1:T(8,128)} %param.8) | copy-start | bytes 884740
  7.2 281.6 %all-reduce.7.cloned.1.call-start = ((), (), s32[]{:S(2)}) async-start(), calls=%async_computation | async-start | bytes 1179648 | tf_op jit(solution)/shard_map/psum | solution.py:20
  10.6 1.1 copy-start.4
  10.7 609.9 %all-reduce.9.cloned.1.call-start = ((), (), s32[]{:S(2)}) async-start(), calls=%async_computation.1 | async-start | bytes 1179648 | tf_op jit(solution)/shard_map/psum | solution.py:20
  288.7 1.4 copy-start.2
  353.4 38.4 %copy-start.3 = (f32[1,384,384]{2,1,0:T(8,128)S(1)}, f32[1,384,384]{2,1,0:T(8,128)}, u32[]{:S(2)}) copy-start(f32[1,384,384]{2,1,0:T(8,128)} %param.6) | copy-start | bytes 1769476
  393.1 0.8 copy-start.5
  653.8 20.6 %copy-start.1 = (f32[384,384]{1,0:T(8,128)S(1)}, f32[384,384]{1,0:T(8,128)}, u32[]{:S(2)}) copy-start(f32[384,384]{1,0:T(8,128)} %all-reduce.9.cloned.1.call-done) | copy-start | bytes 1769476
  940.6 1.0 copy-start.6
Sparse Core Ops, SparseCore 0:
  13.0 275.6 all-reduce.6
  353.5 267.0 all-reduce.8
where the time goes:
time: 960 us; the launch traced here: 950 us
  waiting for transfers between devices  501 us (52%)
  other arithmetic  380 us (40%)
  matrix products  31.6 us (3%)
  between operations  25.2 us (3%)
  local copies, waits for them, and re-layouts  12.1 us (1%)
    psum x2, waiting for transfers between devices, reduce_all(): return lax.psum((summands[0],), ('wide', 'narrow'))  501 us
    another operation x42, other arithmetic, orthonormal(): factor = jnp.linalg.cholesky(square)  173 us
    another operation x26, other arithmetic, orthonormal(): return jax.scipy.linalg.solve_triangular(factor, block.T, lower=True).T  120 us
    another operation x10, other arithmetic, shards(): lower_factor = jnp.linalg.cholesky(gram)  56.7 us
    another operation x3, other arithmetic, shards(): jax.scipy.linalg.solve_triangular(lower_factor, flat_core.T, lower=True)  30.5 us
  transfers between devices with their start and end apart: 2, of which 2 were waited for; matrix products, arithmetic and copies ran while one was open for 5% of the time, Pallas kernels for 0%

commit v1 on v0

v1 whole, which is shorter than its diff:
```python
import functools
import math

import jax
import jax.numpy as jnp
from jax import lax
from jax.experimental import pallas as pl
from jax.experimental.pallas import tpu as pltpu
from jax.sharding import PartitionSpec as P

RANK = 384
HI = lax.Precision.HIGHEST
NN = (((1,), (0,)), ((), ()))
NT = (((1,), (1,)), ((), ()))
TN = (((0,), (0,)), ((), ()))

def dot6(a, b, dims):
    return lax.dot_general(a, b, dims, precision=HI, preferred_element_type=jnp.float32)

def split(a):
    hi = a.astype(jnp.bfloat16)
    return hi, (a - hi.astype(jnp.float32)).astype(jnp.bfloat16)

def dot3(a, b, dims):
    ah, al = a if isinstance(a, tuple) else split(a)
    bh, bl = b if isinstance(b, tuple) else split(b)
    one = lambda x, y: lax.dot_general(x, y, dims, preferred_element_type=jnp.float32)
    return one(ah, bh) + (one(ah, bl) + one(al, bh))

def factor(mats, off):
    n = len(mats[0])
    sub = lax.broadcasted_iota(jnp.int32, (8, 128), 0)
    for t in range(n):
        for A in mats:
            P = A[t]
            c0 = off + 8 * t
            cb = [jnp.broadcast_to(P[:, c0+j:c0+j+1], (8, 128)) for j in range(8)]
            rows, rs, bs = [], [], {}
            dv = None
            for j in range(8):
                dj = jnp.broadcast_to(cb[j][j:j+1, :], (8, 128))
                r = 1.0 / dj
                rowj = jnp.broadcast_to(P[j:j+1, :], (8, 128))
                dv = dj if j == 0 else jnp.where(sub == j, dj, dv)
                rows.append(rowj); rs.append(r)
                m = jnp.where(sub > j, cb[j] * r, 0.0)
                P = P - m * rowj
                for i in range(j+1, 8):
                    b = jnp.broadcast_to(cb[j][i:i+1, :], (8, 128))
                    bs[(j, i)] = b
                    cb[i] = cb[i] - m * b
            A[t] = P * lax.rsqrt(dv)
            for u in range(t+1, n):
                X = A[u]
                cu = [jnp.broadcast_to(X[:, c0+j:c0+j+1], (8, 128)) for j in range(8)]
                for j in range(8):
                    m = cu[j] * rs[j]
                    X = X - m * rows[j]
                    for i in range(j+1, 8):
                        cu[i] = cu[i] - m * bs[(j, i)]
                A[u] = X
    return mats

def with_eye(s, off):
    row = lax.broadcasted_iota(jnp.int32, (64, 128), 0)
    col = lax.broadcasted_iota(jnp.int32, (64, 128), 1)
    eye = jnp.where(col == row + (64 - off), 1.0, 0.0)
    half = (col >= 64) if off else (col < 64)
    a = jnp.where(half, s, eye)
    return [a[8*t:8*t+8, :] for t in range(8)]

def inverses(mats, off):
    done = factor(mats, off)
    return [jnp.concatenate(m, axis=0)[:, 64 - off:128 - off] for m in done]

def body(scale, g_ref, m_ref, s_ref, c_ref, w_ref, co_ref, no_ref, r_ref, kh_ref, kl_ref, y_ref, p1_ref, p2_ref, f_ref, *a_refs):
    ds, dm, dg, dl = dot6, dot3, dot3, dot3
    for q in range(6):
        a_refs[q][...] = g_ref[64*q:64*q+64, :]
    r_ref[...] = jnp.zeros_like(r_ref)
    g = g_ref[...]
    k = ds(g, m_ref[...], NN)
    h = ds(k, g, NN)
    for x, lo in ((k, 0), (h, 384)):
        xh, xl = split(x)
        kh_ref[:, lo:lo+384] = xh
        kl_ref[:, lo:lo+384] = xl
    for p in range(6):
        o = 128 * (p // 2)
        off = 64 * (p % 2)
        (li,) = inverses([with_eye(a_refs[p][:, o:o+128], off)], off)
        rp = ds(li, a_refs[p][:, o:], NN)
        if off:
            col = lax.broadcasted_iota(jnp.int32, rp.shape, 1)
            rp = jnp.where(col >= 64, rp, 0.0)
        r_ref[64*p:64*p+64, o:] = rp
        if p < 5:
            for q in range(p+1, 6):
                oq = 128 * (q // 2)
                lq = rp[:, 64*q-o:64*q-o+64]
                a_refs[q][:, oq:] -= ds(lq, rp[:, oq-o:], TN)
    z0 = ds(ds(s_ref[...], r_ref[...], NN), m_ref[...], NN)
    y_ref[:, :384] = z0
    y_ref[:, 384:] = ds(z0, g_ref[...], NN)
    p1_ref[...] = jnp.zeros_like(p1_ref)
    p2_ref[...] = jnp.zeros_like(p2_ref)

    def wave(w, _):
        y = [y_ref[64*j:64*j+64, :] for j in range(3)]
        prev1, prev2 = p1_ref[...], p2_ref[...]
        z = [v[:, :384] for v in y]
        u = [v[:, 384:] for v in y]
        ss, cs = [], [None]
        s0 = dg(u[0], jnp.concatenate([prev1[:, :384], z[0]], axis=0), NT)
        e1 = dg(u[1], jnp.concatenate([prev1[:, :384], z[1]], axis=0), NT)
        e2 = dg(u[2], prev2[:, :384], NT)
        s2 = dg(u[2], jnp.concatenate([prev1[:, :384], z[2]], axis=0), NT)
        c1 = e1[:, :64]
        c1w = jnp.concatenate([c1, c1], axis=0)
        s1 = e1 - dg(c1, c1w, NT)
        e2w = jnp.concatenate([e2, e2], axis=0)
        s2 = s2 - dg(e2, e2w, NT)
        li = inverses([with_eye(s, 64) for s in (s0, s1, s2)], 64)
        x = [y[0], y[1] - dg(c1, prev1, NN), y[2] - dg(e2, prev2, NN)]
        n = [dl(li[j], x[j], NN) for j in range(3)]
        p2_ref[0:64, :] = prev1
        p2_ref[64:128, :] = n[1]
        p1_ref[...] = n[0]
        for j in range(3):
            @pl.when(w - j < 6)
            def _(j=j):
                f_ref[64*j:64*j+64, :] = n[j]
        nz = jnp.concatenate([v[:, :384] for v in n], axis=0)
        ny = dm(nz, (kh_ref[...], kl_ref[...]), NN)
        for j in range(3):
            @pl.when(w >= j)
            def _(j=j):
                y_ref[64*j:64*j+64, :] = ny[64*j:64*j+64, :]
        return 0

    lax.fori_loop(0, 8, wave, 0)
    co_ref[...] = scale * dot3(f_ref[:, :384], c_ref[0], NT)
    no_ref[:, 0, :] = dot3(f_ref[:, 384:], w_ref[:, 0, :], NN)

def finish(g, m, st, core, nxt, scale):
    v = pl.BlockSpec(memory_space=pltpu.VMEM)
    return pl.pallas_call(
        functools.partial(body, scale),
        out_shape=(jax.ShapeDtypeStruct((192, 384), jnp.float32), jax.ShapeDtypeStruct((192, 1, 384), jnp.float32)),
        in_specs=[v] * 5, out_specs=(v, v),
        scratch_shapes=[pltpu.VMEM((384, 384), jnp.float32), pltpu.VMEM((384, 768), jnp.bfloat16), pltpu.VMEM((384, 768), jnp.bfloat16),
            pltpu.VMEM((192, 768), jnp.float32), pltpu.VMEM((64, 768), jnp.float32), pltpu.VMEM((128, 768), jnp.float32),
            pltpu.VMEM((192, 768), jnp.float32)] + [pltpu.VMEM((64, 384), jnp.float32)] * 6,
        compiler_params=pltpu.CompilerParams(vmem_limit_bytes=48 * 1024 * 1024),
    )(g, m, st, core, nxt)


MESH = pl.DeviceIdType.MESH
PAIRS = ((0, 0), (0, 1), (0, 2), (1, 1), (1, 2), (2, 2))


def reduce_body(core_ref, next_ref, g_ref, m_ref, acc, r1, s1, r2, s2, r3, r4, res, send_sem, recv_sem):
    wide, y = lax.axis_index("wide"), lax.axis_index("narrow")
    core, z, x = lax.rem(wide, 2), lax.rem(wide // 2, 8), wide // 16

    def place(x, y, z, core):
        return ((x * 8 + z) * 2 + core, y)

    sibling = place(x, y, z, 1 - core)
    along_x = [place(lax.rem(x + d, 4), y, z, core) for d in range(1, 4)]
    along_y = [place(x, lax.rem(y + d, 8), z, core) for d in range(1, 8)]
    along_z = [place(x, y, lax.rem(z + d, 8), core) for d in range(1, 8)]

    barrier = pltpu.get_barrier_semaphore()
    for other in [sibling] + along_x + along_y + along_z:
        pl.semaphore_signal(barrier, inc=1, device_id=other, device_id_type=MESH)

    c = split(core_ref[0])
    w = split(next_ref[:, 0, :])
    gram = dot3(c, c, TN)
    cross = dot3(w, w, NT)
    for b, (i, j) in enumerate(PAIRS):
        for k, a in ((0, gram), (6, cross)):
            block = a[128*i:128*i+128, 128*j:128*j+128]
            acc[16*(b+k):16*(b+k)+16] = block.reshape(16, 8, 128)
    pl.semaphore_wait(barrier, 18)

    count = [0]

    def copy(src, dst, other):
        n = count[0]
        count[0] += 1
        d = pltpu.make_async_remote_copy(src_ref=src, dst_ref=dst, send_sem=send_sem.at[n], recv_sem=recv_sem.at[n],
                                         device_id=other, device_id_type=MESH)
        d.start()
        return d

    sent = [copy(acc.at[pl.ds(96 * (1 - core), 96)], r1, sibling)]
    sent[0].wait_recv()
    s1[...] = acc[pl.ds(96 * core, 96)] + r1[...]

    step = [copy(s1.at[pl.ds(24 * lax.rem(x + d, 4), 24)], r2.at[d-1], along_x[d-1]) for d in (2, 1, 3)]
    for d in step:
        d.wait_recv()
    sent += step
    s2[...] = s1[pl.ds(24 * x, 24)] + r2[0] + (r2[1] + r2[2])

    step = [copy(s2.at[pl.ds(3 * lax.rem(y + d, 8), 3)], r3.at[d-1], along_y[d-1]) for d in (4, 3, 5, 2, 6, 1, 7)]
    for d in step:
        d.wait_recv()
    sent += step
    total = s2[pl.ds(3 * y, 3)]
    for d in range(7):
        total = total + r3[d]
    r4[z] = total

    step = [copy(r4.at[z], r4.at[z], along_z[d-1]) for d in (4, 3, 5, 2, 6, 1, 7)]
    for d in step:
        d.wait_recv()
    sent += step
    total = r4[0]
    for d in range(1, 8):
        total = total + r4[d]
    at = 96 * core + 24 * x + 3 * y
    res[pl.ds(at, 3)] = total

    mine = res.at[pl.ds(at, 3)]
    step = [copy(mine, mine, along_y[d-1]) for d in (4, 3, 5, 2, 6, 1, 7)]
    for d in step:
        d.wait_recv()
    sent += step
    mine = res.at[pl.ds(96 * core + 24 * x, 24)]
    step = [copy(mine, mine, along_x[d-1]) for d in (2, 1, 3)]
    for d in step:
        d.wait_recv()
    sent += step
    mine = res.at[pl.ds(96 * core, 96)]
    step = [copy(mine, mine, sibling)]
    step[0].wait_recv()
    sent += step
    for b, (i, j) in enumerate(PAIRS):
        for k, out in ((0, g_ref), (6, m_ref)):
            block = res[16*(b+k):16*(b+k)+16].reshape(128, 128)
            out[128*i:128*i+128, 128*j:128*j+128] = block
            if i < j:
                out[128*j:128*j+128, 128*i:128*i+128] = block.T
    for d in sent:
        d.wait_send()


def reduced(core, nxt):
    v = pl.BlockSpec(memory_space=pltpu.VMEM)
    tile = lambda *lead: pltpu.VMEM(lead + (8, 128), jnp.float32)
    square = jax.ShapeDtypeStruct((RANK, RANK), jnp.float32)
    return pl.pallas_call(
        reduce_body,
        out_shape=(square, square),
        in_specs=[v, v], out_specs=(v, v),
        scratch_shapes=[tile(192), tile(96), tile(96), tile(3, 24), tile(24), tile(7, 3), tile(8, 3), tile(192),
                        pltpu.SemaphoreType.DMA((29,)), pltpu.SemaphoreType.DMA((29,))],
        compiler_params=pltpu.CompilerParams(collective_id=0, has_side_effects=True, vmem_limit_bytes=48 * 1024 * 1024),
    )(core, nxt)


def shards(core, next_core, start_block):
    gram, cross = reduced(core, next_core)
    scale = math.sqrt(core.shape[0] * lax.axis_size("wide") * lax.axis_size("narrow") * core.shape[1])
    core_t, next_out = finish(gram, cross, start_block.T, core, next_core, scale)
    return core_t.T[None], next_out


def solution(mesh):
    placed = (P(("wide", "narrow"), None, None), P(None, ("wide", "narrow"), None), P())
    return jax.shard_map(
        shards,
        mesh=mesh,
        in_specs=placed,
        out_specs=(P(("wide", "narrow"), None, None), P(None, ("wide", "narrow"), None)),
        check_vma=False,
    )
```

time: 960 us -> 101 us (0.11); the launches traced: 950 us -> 101 us
  waiting for transfers between devices: 501 us -> 0 us
  other arithmetic: 380 us -> 0 us
  Pallas kernels: 0 us -> 98.5 us
  matrix products: 31.6 us -> 0 us
  between operations: 25.2 us -> 0.66 us
  local copies, waits for them, and re-layouts: 12.1 us -> 2.12 us
    psum x2 -> x0, waiting for transfers between devices: 501 us -> none  [reduce_all(): return lax.psum((summands[0],), ('wide', 'narrow'))]
    another operation x81 -> x0, other arithmetic: 380 us -> none  [the longest x42 173 us: orthonormal(): factor = jnp.linalg.cholesky(square)]
    pallas_call x0 -> x2, Pallas kernels: none -> 98.5 us  [the longest x1 53.4 us: finish(): pl.pallas_call(functools.partial(body, scale), out_shape=(jax.ShapeDtypeS...]
    dot_general x19 -> x0, matrix products: 20.5 us -> none  [the longest x6 5.89 us: shards(): jnp.dot(bond_gram, basis, precision=highest, preferred_element_type=jnp.f...]
    another operation x39 -> x0, matrix products: 11.1 us -> none  [the longest x18 5.44 us: orthonormal(): return jax.scipy.linalg.solve_triangular(factor, block.T, lower=True).T]
  transfers between devices with their start and end apart: 2 -> 0, of which waited for: 2 -> 0; matrix products, arithmetic and copies ran while one was open for 5% -> 0% of each run, Pallas kernels for 0% -> 0%
where the time goes in v1:
time: 101 us
  Pallas kernels  98.5 us (98%)
  local copies, waits for them, and re-layouts  2.12 us (2%)
    pallas_call x1, Pallas kernels, finish(): pl.pallas_call(functools.partial(body, scale), out_shape=(jax.ShapeDtypeS...  53.4 us
    pallas_call x1, Pallas kernels, reduced(): pl.pallas_call(reduce_body, out_shape=(square, square), in_specs=[v, v],...  45.1 us
    unnamed x6, local copies, waits for them, and re-layouts  2.12 us

profile of v1, /device:TPU:1, one launch (start us, length us, event | category | flops | bytes accessed | tf_op | source)
XLA Modules:
  0.0 101.3 jit_solution(9057981637714147802)
XLA Ops:
  0.6 0.0 copy-start
  0.6 1.1 %copy-done = f32[1,384,384]{2,1,0:T(8,128)S(1)} copy-done((f32[1,384,384]{2,1,0:T(8,128)S(1)}, f32[1,384,384]{2,1,0:T(8,128)}, u32[]{:S(2)}) %copy-start) | copy-done | bytes 589848
  1.7 0.0 copy-start.1
  1.7 1.1 %copy-done.1 = f32[384,1,384]{2,1,0:T(1,128)S(1)} copy-done((f32[384,1,384]{2,1,0:T(1,128)S(1)}, f32[384,1,384]{2,1,0:T(1,128)}, u32[]{:S(2)}) %copy-start.1) | copy-done | bytes 589848
  2.8 0.0 copy-start.2
  2.8 45.1 %shard_map.50 = (f32[384,384]{1,0:T(8,128)S(1)}, f32[384,384]{1,0:T(8,128)S(1)}) custom-call(f32[1,384,384]{2,1,0:T(8,128)S(1)} %copy-done, f32[384,1,384]{2,1,0:T(1,128)S(1)} %copy-done.1), custom_call_target="tpu_custom_call" | custom-call | tf_op jit(solution)/shard_map/pallas_call | solution.py:255
  47.8 0.0 copy-done.2
  47.8 53.4 %shard_map.51 = (f32[192,384]{1,0:T(8,128)}, f32[192,1,384]{2,1,0:T(1,128)}) custom-call(f32[384,384]{1,0:T(8,128)S(1)} %get-tuple-element.6.g_ref, f32[384,384]{1,0:T(8,128)S(1)} %get-tuple-element.7.m_ref, f32[192,384]{1,0:T(8,128)S(1)} %bitcast.4, f32[1,384,384]{2,1,0:T(8,128)S(1)} %copy-done, f32[384,1,384]{2,1,0:T(1,128)S(1)} %copy-done.1), custom_call_target="tpu_custom_call" | custom-call | tf_op jit(solution)/shard_map/pallas_call | solution.py:147
Async XLA Ops:
  0.6 1.1 %copy-start = (f32[1,384,384]{2,1,0:T(8,128)S(1)}, f32[1,384,384]{2,1,0:T(8,128)}, u32[]{:S(2)}) copy-start(f32[1,384,384]{2,1,0:T(8,128)} %c_ref.1) | copy-start | bytes 1769476
  1.7 1.1 %copy-start.1 = (f32[384,1,384]{2,1,0:T(1,128)S(1)}, f32[384,1,384]{2,1,0:T(1,128)}, u32[]{:S(2)}) copy-start(f32[384,1,384]{2,1,0:T(1,128)} %w_ref.1) | copy-start | bytes 1769476
  2.8 45.1 %copy-start.2 = (f32[384,192]{0,1:T(8,128)S(1)}, f32[384,192]{0,1:T(8,128)}, u32[]{:S(2)}) copy-start(f32[384,192]{0,1:T(8,128)} %param.5) | copy-start | bytes 884740

commit v2 on v0

v2 whole, which is shorter than its diff:
```python
import functools
import math

import jax
import jax.numpy as jnp
from jax import lax
from jax.experimental import pallas as pl
from jax.experimental.pallas import tpu as pltpu
from jax.sharding import PartitionSpec as P

RANK = 384
ITERS = 6
MESH = pl.DeviceIdType.MESH
PAIRS = ((0, 0), (0, 1), (0, 2), (1, 1), (1, 2), (2, 2))
HI = lax.Precision.HIGHEST
NN = (((1,), (0,)), ((), ()))
NT = (((1,), (1,)), ((), ()))
TN = (((0,), (0,)), ((), ()))


def dot6(a, b, dims):
    return lax.dot_general(a, b, dims, precision=HI, preferred_element_type=jnp.float32)


def split(a):
    hi = a.astype(jnp.bfloat16)
    return hi, (a - hi.astype(jnp.float32)).astype(jnp.bfloat16)


def dot3(a, b, dims):
    ah, al = a if isinstance(a, tuple) else split(a)
    bh, bl = b if isinstance(b, tuple) else split(b)
    one = lambda x, y: lax.dot_general(x, y, dims, preferred_element_type=jnp.float32)
    if dims == TN:
        return one(ah, bh) + (one(ah, bl) + one(al, bh))
    rows = ah.shape[0]
    both = one(jnp.concatenate([ah, al], axis=0), bh)
    return both[:rows] + (both[rows:] + one(ah, bl))


def row_of(v, j):
    return jnp.broadcast_to(v[j:j+1, :], (8, 128))


def factor(groups, gj):
    sub = lax.broadcasted_iota(jnp.int32, (8, 128), 0)
    lane_id = lax.broadcasted_iota(jnp.int32, (8, 128), 1)
    n = 8

    def lanes(pair, X, t):
        if not pair:
            return [jnp.broadcast_to(X[:, 64+8*t+j:64+8*t+j+1], (8, 128)) for j in range(8)]
        base = jnp.where(lane_id < 64, 0, 64)
        return [jnp.take_along_axis(X, base + (8*t + j), axis=1) for j in range(8)]

    ahead = [lanes(pair, tiles[0][0], 0) for pair, tiles in groups]
    for t in range(n):
        for g, (pair, A) in enumerate(groups):
            cb = ahead[g]
            P = A[t]
            W = list(P)
            dv = rv = None
            last = t + 1 == n
            if not last:
                X = A[t+1]
                cu = lanes(pair, X[0], t)
                cn = lanes(pair, X[0], t+1)
            others = range(t+2, n)
            if not gj:
                co = {u: lanes(pair, A[u][0], t) for u in others}
            for j in range(8):
                dj = row_of(cb[j], j)
                r = 1.0 / dj
                dv = dj if j == 0 else jnp.where(sub == j, dj, dv)
                rows = [row_of(p, j) for p in P]
                bs = {i: row_of(cb[j], i) for i in range(j+1, 8)}
                if gj:
                    rv = r if j == 0 else jnp.where(sub == j, r, rv)
                    mg = jnp.where(sub == j, 0.0, cb[j] * r)
                    W = [w - mg * x for w, x in zip(W, rows)]
                    mf = jnp.where(sub > j, mg, 0.0)
                else:
                    mg = mf = jnp.where(sub > j, cb[j] * r, 0.0)
                P = [p - mf * x for p, x in zip(P, rows)]
                for i in range(j+1, 8):
                    cb[i] = cb[i] - mg * bs[i]
                if not last:
                    m = cu[j] * r
                    X = [a - m * x for a, x in zip(X, rows)]
                    for i in range(8):
                        cn[i] = cn[i] - m * row_of(cu[j], i)
                    for i in range(j+1, 8):
                        cu[i] = cu[i] - m * bs[i]
                if not gj:
                    for u in others:
                        m = co[u][j] * r
                        A[u] = [a - m * x for a, x in zip(A[u], rows)]
                        for i in range(j+1, 8):
                            co[u][i] = co[u][i] - m * bs[i]
            s = lax.rsqrt(dv)
            A[t] = [p * s for p in P]
            if not last:
                A[t+1] = X
                ahead[g] = cn
            if gj and t + 2 < n:
                wr = [[row_of(w * rv, j) for j in range(8)] for w in W]
                for u in others:
                    co = lanes(pair, A[u][0], t)
                    new = []
                    for a, wv in zip(A[u], wr):
                        p = [co[j] * wv[j] for j in range(8)]
                        new.append(a - (((p[0] + p[1]) + (p[2] + p[3])) + ((p[4] + p[5]) + (p[6] + p[7]))))
                    A[u] = new
    return groups


def iotas(rows):
    return lax.broadcasted_iota(jnp.int32, (rows, 128), 0), lax.broadcasted_iota(jnp.int32, (rows, 128), 1)


def single(s):
    row, col = iotas(64)
    a = jnp.where(col >= 64, s, jnp.where(col == row, 1.0, 0.0))
    return False, [[a[8*t:8*t+8, :]] for t in range(8)]


def pair(s):
    row, col = iotas(64)
    eye = jnp.where((col == row) | (col == row + 64), 1.0, 0.0)
    return True, [[s[8*t:8*t+8, :], eye[8*t:8*t+8, :]] for t in range(8)]


def inverse(group):
    is_pair, tiles = group
    a = jnp.concatenate([t[-1] for t in tiles], axis=0)
    if not is_pair:
        return a[:, :64]
    row, col = iotas(128)
    return jnp.where((row < 64) == (col < 64), jnp.concatenate([a, a], axis=0), 0.0)


def sum_and_factor(core_hbm, next_hbm, r_ref, m_ref, ortho_ref, moved_ref, c_ref, w_ref, acc, r1, s1, r2, r4, res, *more):
    a_refs, t_refs = more[:6], more[6:12]
    in_sem, pair_send, pair_recv, plane_send, plane_recv, line_send, line_recv = more[12:]
    wide, y = lax.axis_index("wide"), lax.axis_index("narrow")
    core, z, x = lax.rem(wide, 2), lax.rem(wide // 2, 8), wide // 16

    def place(x, y, z, core):
        return ((x * 8 + z) * 2 + core, y)

    def in_plane(d):
        return lax.rem(x + d // 8, 4), lax.rem(z + lax.rem(d, 8), 8)

    sibling = place(x, y, z, 1 - core)
    along_y = [place(x, lax.rem(y + d, 8), z, core) for d in range(1, 8)]

    load_c = pltpu.make_async_copy(core_hbm, c_ref, in_sem.at[0])
    load_c.start()
    load_w = pltpu.make_async_copy(next_hbm, w_ref, in_sem.at[1])
    load_w.start()

    barrier = pltpu.get_barrier_semaphore()
    for other in [sibling] + along_y:
        pl.semaphore_signal(barrier, inc=1, device_id=other, device_id_type=MESH)

    def greet(d, _):
        px, pz = in_plane(d)
        pl.semaphore_signal(barrier, inc=1, device_id=place(px, y, pz, core), device_id_type=MESH)
        return 0

    lax.fori_loop(1, 32, greet, 0)

    def remote(src, dst, send, recv, other):
        return pltpu.make_async_remote_copy(src_ref=src, dst_ref=dst, send_sem=send, recv_sem=recv, device_id=other, device_id_type=MESH)

    def fill(k, a):
        for b, (i, j) in enumerate(PAIRS):
            acc[k, 32*b:32*b+32] = a[128*i:128*i+128, 128*j:128*j+128].reshape(32, 4, 128)

    def pair_out(k):
        return remote(acc.at[k, pl.ds(96 * (1 - core), 96)], r1.at[k], pair_send.at[0, k], pair_recv.at[0, k], sibling)

    def pair_back(k):
        mine = res.at[k, pl.ds(96 * core, 96)]
        return remote(mine, mine, pair_send.at[1, k], pair_recv.at[1, k], sibling)

    def plane_out(k, d):
        px, pz = in_plane(d)
        return remote(s1.at[k, pl.ds(3 * (px * 8 + pz), 3)], r2.at[k, d - 1], plane_send.at[0, k, d - 1], plane_recv.at[0, k, d - 1],
                      place(px, y, pz, core))

    at = 96 * core + 3 * (x * 8 + z)

    def plane_back(k, d):
        px, pz = in_plane(d)
        mine = res.at[k, pl.ds(at, 3)]
        return remote(mine, mine, plane_send.at[1, k, d - 1], plane_recv.at[1, k, d - 1], place(px, y, pz, core))

    def line(k, d):
        return remote(r4.at[k, y], r4.at[k, y], line_send.at[k, d - 1], line_recv.at[k, d - 1], along_y[d - 1])

    def each(what):
        def step(d, _):
            what(d)
            return 0

        lax.fori_loop(1, 32, step, 0)

    def pair_sum(k):
        pair_out(k).wait_recv()
        s1[k] = acc[k, pl.ds(96 * core, 96)] + r1[k]
        each(lambda d: plane_out(k, d).start())

    def plane_sum(k):
        each(lambda d: plane_out(k, d).wait_recv())
        total = s1[k, pl.ds(3 * (x * 8 + z), 3)]
        parts = [r2[k, d] for d in range(31)]
        while len(parts) > 1:
            parts = [a + b for a, b in zip(parts[::2], parts[1::2])] + ([parts[-1]] if len(parts) % 2 else [])
        r4[k, y] = total + parts[0]
        for d in (4, 3, 5, 2, 6, 1, 7):
            line(k, d).start()

    def line_sum(k):
        for d in range(1, 8):
            line(k, d).wait_recv()
        p = [r4[k, d] for d in range(8)]
        res[k, pl.ds(at, 3)] = ((p[0] + p[1]) + (p[2] + p[3])) + ((p[4] + p[5]) + (p[6] + p[7]))
        each(lambda d: plane_back(k, d).start())

    def gathered(k):
        each(lambda d: plane_back(k, d).wait_recv())
        pair_back(k).start()

    load_c.wait()
    c = split(c_ref[0])
    fill(0, dot3(c, c, TN))
    pl.semaphore_wait(barrier, 39)
    pair_out(0).start()
    load_w.wait()
    w = split(w_ref[:, 0, :])
    fill(1, dot3(w, w, NT))
    pair_out(1).start()
    pair_sum(0)
    turned = c_ref[0].T
    for q in range(6):
        t_refs[q][...] = turned[64*q:64*q+64, :]
    r_ref[...] = jnp.zeros_like(r_ref)
    pair_sum(1)
    plane_sum(0)
    plane_sum(1)
    line_sum(0)
    line_sum(1)
    gathered(0)
    pair_back(0).wait_recv()

    def block(k, b):
        return res[k, 32*b:32*b+32].reshape(128, 128)

    for b, (i, j) in enumerate(PAIRS):
        a = block(0, b)
        a_refs[2*i][:, 128*j:128*j+128] = a[:64]
        a_refs[2*i+1][:, 128*j:128*j+128] = a[64:]
    for p in range(6):
        o = 128 * (p // 2)
        d = a_refs[p][:, o:o+128]
        if p % 2 == 0:
            d = pltpu.roll(d, 64, 1)
        (g,) = factor([single(d)], False)
        li = inverse(g)
        rp = dot6(li, a_refs[p][:, o:], NN)
        if p % 2:
            rp = jnp.where(lax.broadcasted_iota(jnp.int32, rp.shape, 1) >= 64, rp, 0.0)
        r_ref[64*p:64*p+64, o:] = rp
        ortho = dot3(li, t_refs[p][...], NN)
        ortho_ref[64*p:64*p+64, :] = ortho
        for q in range(p + 1, 6):
            oq = 128 * (q // 2)
            lq = rp[:, 64*q-o:64*q-o+64]
            a_refs[q][:, oq:] -= dot6(lq, rp[:, oq-o:], TN)
            t_refs[q][...] -= dot3(lq, ortho, TN)
        moved_ref[64*p:64*p+64, :] = dot3(rp, (w[0][o:, :], w[1][o:, :]), NN)
        if p == 1:
            gathered(1)
    pair_back(1).wait_recv()
    for b, (i, j) in enumerate(PAIRS):
        a = block(1, b)
        m_ref[128*i:128*i+128, 128*j:128*j+128] = a
        if i < j:
            m_ref[128*j:128*j+128, 128*i:128*i+128] = a.T
    for k in range(2):
        pair_out(k).wait_send()
        each(lambda d: plane_out(k, d).wait_send())
        for d in range(1, 8):
            line(k, d).wait_send()
        each(lambda d: plane_back(k, d).wait_send())
        pair_back(k).wait_send()


def first(core, nxt):
    v = pl.BlockSpec(memory_space=pltpu.VMEM)
    anywhere = pl.BlockSpec(memory_space=pl.ANY)
    f32 = lambda *s: pltpu.VMEM(s, jnp.float32)
    half = lambda *lead: pltpu.VMEM(lead + (4, 128), jnp.float32)
    sems = pltpu.SemaphoreType.DMA
    square = jax.ShapeDtypeStruct((RANK, RANK), jnp.float32)
    return pl.pallas_call(
        sum_and_factor,
        out_shape=(square,) * 4,
        in_specs=[anywhere] * 2, out_specs=(v,) * 4,
        scratch_shapes=[f32(1, RANK, RANK), f32(RANK, 1, RANK), half(2, 192), half(2, 96), half(2, 96), half(2, 31, 3), half(2, 8, 3), half(2, 192)]
        + [f32(64, RANK)] * 12
        + [sems((2,)), sems((2, 2)), sems((2, 2)), sems((2, 2, 31)), sems((2, 2, 31)), sems((2, 7)), sems((2, 7))],
        compiler_params=pltpu.CompilerParams(collective_id=0, has_side_effects=True, vmem_limit_bytes=40 * 1024 * 1024),
    )(core, nxt)


def iterate(scale, r_ref, m_ref, ortho_ref, moved_ref, s_ref, co_ref, no_ref, bh_ref, bl_ref, y_ref, p1_ref, p2_ref, f_ref):
    r = r_ref[...]
    rm = dot6(r, m_ref[...], NN)
    y_ref[...] = dot6(dot6(s_ref[...], rm, NN), r, NT)
    bh_ref[...], bl_ref[...] = split(dot6(rm, r, NT))
    p1_ref[...] = jnp.zeros_like(p1_ref)
    p2_ref[...] = jnp.zeros_like(p2_ref)

    def wave(w, _):
        y = [y_ref[64*j:64*j+64, :] for j in range(3)]
        ys = [split(v) for v in y]
        prev1, prev2 = p1_ref[...], p2_ref[...]
        p1s, p2s = split(prev1), split(prev2)
        stack = lambda *parts: tuple(jnp.concatenate([q[i] for q in parts], axis=0) for i in range(2))
        left = lambda q: (q[0][:, :RANK], q[1][:, :RANK])
        e0 = dot3(ys[0], stack(ys[0], ys[1]), NT)
        e1 = dot3(ys[1], stack(left(p1s), ys[1]), NT)
        e2 = dot3(ys[2], stack(left(p2s), ys[2], ys[2]), NT)
        c1, c2 = split(e1[:, :64]), split(e2[:, :128])
        s1 = e1 - dot3(c1, stack(c1, c1), NT)
        s2 = e2[:, 128:] - dot3(c2, stack(c2, c2), NT)
        col = lax.broadcasted_iota(jnp.int32, (64, 128), 1)
        g01, g2 = factor([pair(jnp.where(col < 64, e0, s1)), single(s2)], True)
        image = dot3(stack(*ys), (bh_ref[...], bl_ref[...]), NN)
        both = [jnp.concatenate([y[j], image[64*j:64*j+64]], axis=1) for j in range(3)]
        x1 = both[1] - dot3(c1, p1s, NN)
        x2 = both[2] - dot3(c2, p2s, NN)
        n01 = dot3(inverse(g01), jnp.concatenate([both[0], x1], axis=0), NN)
        n2 = dot3(inverse(g2), x2, NN)
        n = [n01[:64], n01[64:], n2]
        p2_ref[0:64, :] = prev1
        p2_ref[64:128, :] = n[1]
        p1_ref[...] = n[0]
        for j in range(3):
            @pl.when(w - j < ITERS)
            def _(j=j):
                f_ref[64*j:64*j+64, :] = n[j][:, :RANK]

            @pl.when(w >= j)
            def _(j=j):
                y_ref[64*j:64*j+64, :] = n[j][:, RANK:]
        return 0

    lax.fori_loop(0, ITERS + 2, wave, 0)
    f = split(f_ref[...])
    co_ref[...] = scale * dot3(f, ortho_ref[...], NN)
    no_ref[:, 0, :] = dot3(f, moved_ref[...], NN)


def second(r, m, ortho, moved, start, scale):
    v = pl.BlockSpec(memory_space=pltpu.VMEM)
    f32 = lambda *s: pltpu.VMEM(s, jnp.float32)
    bf16 = lambda *s: pltpu.VMEM(s, jnp.bfloat16)
    return pl.pallas_call(
        functools.partial(iterate, scale),
        out_shape=(jax.ShapeDtypeStruct((192, RANK), jnp.float32), jax.ShapeDtypeStruct((192, 1, RANK), jnp.float32)),
        in_specs=[v] * 5, out_specs=(v, v),
        scratch_shapes=[bf16(RANK, RANK), bf16(RANK, RANK), f32(192, RANK), f32(64, 2 * RANK), f32(128, 2 * RANK), f32(192, RANK)],
        compiler_params=pltpu.CompilerParams(vmem_limit_bytes=40 * 1024 * 1024),
    )(r, m, ortho, moved, start)


def shards(core, next_core, start_block):
    r, m, ortho, moved = first(core, next_core)
    scale = math.sqrt(core.shape[0] * lax.axis_size("wide") * lax.axis_size("narrow") * core.shape[1])
    core_t, next_out = second(r, m, ortho, moved, start_block.T, scale)
    return core_t.T[None], next_out


def solution(mesh):
    placed = (P(("wide", "narrow"), None, None), P(None, ("wide", "narrow"), None), P())
    return jax.shard_map(
        shards,
        mesh=mesh,
        in_specs=placed,
        out_specs=(P(("wide", "narrow"), None, None), P(None, ("wide", "narrow"), None)),
        check_vma=False,
    )
```

time: 960 us -> 88.6 us (0.09); the launches traced: 950 us -> 88.4 us
  waiting for transfers between devices: 501 us -> 0 us
  other arithmetic: 380 us -> 0 us
  Pallas kernels: 0 us -> 85.7 us
  matrix products: 31.6 us -> 0 us
  between operations: 25.2 us -> 0.66 us
  local copies, waits for them, and re-layouts: 12.1 us -> 2.12 us
    psum x2 -> x0, waiting for transfers between devices: 501 us -> none  [reduce_all(): return lax.psum((summands[0],), ('wide', 'narrow'))]
    another operation x81 -> x0, other arithmetic: 380 us -> none  [the longest x42 173 us: orthonormal(): factor = jnp.linalg.cholesky(square)]
    pallas_call x0 -> x2, Pallas kernels: none -> 85.7 us  [the longest x1 58.1 us: first(): pl.pallas_call(sum_and_factor, out_shape=(square,) * 4, in_specs=[anywher...]
    dot_general x19 -> x0, matrix products: 20.5 us -> none  [the longest x6 5.89 us: shards(): jnp.dot(bond_gram, basis, precision=highest, preferred_element_type=jnp.f...]
    another operation x39 -> x0, matrix products: 11.1 us -> none  [the longest x18 5.44 us: orthonormal(): return jax.scipy.linalg.solve_triangular(factor, block.T, lower=True).T]
  transfers between devices with their start and end apart: 2 -> 0, of which waited for: 2 -> 0; matrix products, arithmetic and copies ran while one was open for 5% -> 0% of each run, Pallas kernels for 0% -> 0%
where the time goes in v2:
time: 88.6 us; the launch traced here: 88.4 us
  Pallas kernels  85.7 us (97%)
  local copies, waits for them, and re-layouts  2.12 us (2%)
    pallas_call x1, Pallas kernels, first(): pl.pallas_call(sum_and_factor, out_shape=(square,) * 4, in_specs=[anywher...  58.1 us
    pallas_call x1, Pallas kernels, second(): pl.pallas_call(functools.partial(iterate, scale), out_shape=(jax.ShapeDty...  27.5 us
    unnamed x6, local copies, waits for them, and re-layouts  2.12 us

profile of v2, /device:TPU:1, one launch (start us, length us, event | category | flops | bytes accessed | tf_op | source)
XLA Modules:
  0.0 88.4 jit_solution(10267447710693603382)
XLA Ops:
  0.6 0.0 copy-start
  0.6 1.1 %copy-done = f32[1,384,384]{2,1,0:T(8,128)S(1)} copy-done((f32[1,384,384]{2,1,0:T(8,128)S(1)}, f32[1,384,384]{2,1,0:T(8,128)}, u32[]{:S(2)}) %copy-start) | copy-done | bytes 589848
  1.7 0.0 copy-start.1
  1.7 1.1 %copy-done.1 = f32[384,1,384]{2,1,0:T(1,128)S(1)} copy-done((f32[384,1,384]{2,1,0:T(1,128)S(1)}, f32[384,1,384]{2,1,0:T(1,128)}, u32[]{:S(2)}) %copy-start.1) | copy-done | bytes 589848
  2.8 0.0 copy-start.2
  2.8 58.1 %shard_map.50 = (f32[384,384]{1,0:T(8,128)S(1)}, f32[384,384]{1,0:T(8,128)S(1)}, f32[384,384]{1,0:T(8,128)S(1)}, f32[384,384]{1,0:T(8,128)S(1)}) custom-call(f32[1,384,384]{2,1,0:T(8,128)S(1)} %copy-done, f32[384,1,384]{2,1,0:T(1,128)S(1)} %copy-done.1), custom_call_target="tpu_custom_call" | custom-call | tf_op jit(solution)/shard_map/pallas_call | solution.py:307
  60.9 0.0 copy-done.2
  60.9 27.5 %shard_map.51 = (f32[192,384]{1,0:T(8,128)}, f32[192,1,384]{2,1,0:T(1,128)}) custom-call(f32[384,384]{1,0:T(8,128)S(1)} %get-tuple-element.8.r_ref, f32[384,384]{1,0:T(8,128)S(1)} %get-tuple-element.9.m_ref, f32[384,384]{1,0:T(8,128)S(1)} %get-tuple-element.10.ortho_ref, f32[384,384]{1,0:T(8,128)S(1)} %get-tuple-element.11.moved_ref, f32[192,384]{1,0:T(8,128)S(1)} %bitcast.4), custom_call_target="tpu_custom_call" | custom-call | tf_op jit(solution)/shard_map/pallas_call | solution.py:371
Async XLA Ops:
  0.6 1.1 %copy-start = (f32[1,384,384]{2,1,0:T(8,128)S(1)}, f32[1,384,384]{2,1,0:T(8,128)}, u32[]{:S(2)}) copy-start(f32[1,384,384]{2,1,0:T(8,128)} %core_hbm.1) | copy-start | bytes 1769476
  1.7 1.1 %copy-start.1 = (f32[384,1,384]{2,1,0:T(1,128)S(1)}, f32[384,1,384]{2,1,0:T(1,128)}, u32[]{:S(2)}) copy-start(f32[384,1,384]{2,1,0:T(1,128)} %next_hbm.1) | copy-start | bytes 1769476
  2.8 58.1 %copy-start.2 = (f32[384,192]{0,1:T(8,128)S(1)}, f32[384,192]{0,1:T(8,128)}, u32[]{:S(2)}) copy-start(f32[384,192]{0,1:T(8,128)} %param.5) | copy-start | bytes 884740

commit v3 on v2

--- a/solution.py
+++ b/solution.py
@@ -45,7 +45,7 @@
 def factor(groups, gj):
     sub = lax.broadcasted_iota(jnp.int32, (8, 128), 0)
     lane_id = lax.broadcasted_iota(jnp.int32, (8, 128), 1)
-    n = 8
+    n = len(groups[0][1])
 
     def lanes(pair, X, t):
         if not pair:
@@ -125,9 +125,9 @@
 
 
 def pair(s):
-    row, col = iotas(64)
+    row, col = iotas(s.shape[0])
     eye = jnp.where((col == row) | (col == row + 64), 1.0, 0.0)
-    return True, [[s[8*t:8*t+8, :], eye[8*t:8*t+8, :]] for t in range(8)]
+    return True, [[s[8*t:8*t+8, :], eye[8*t:8*t+8, :]] for t in range(s.shape[0] // 8)]
 
 
 def inverse(group):
@@ -135,13 +135,15 @@
     a = jnp.concatenate([t[-1] for t in tiles], axis=0)
     if not is_pair:
         return a[:, :64]
+    if a.shape[0] < 64:
+        a = jnp.concatenate([a, jnp.zeros((64 - a.shape[0], 128), jnp.float32)], axis=0)
     row, col = iotas(128)
     return jnp.where((row < 64) == (col < 64), jnp.concatenate([a, a], axis=0), 0.0)
 
 
-def sum_and_factor(core_hbm, next_hbm, r_ref, m_ref, ortho_ref, moved_ref, c_ref, w_ref, acc, r1, s1, r2, r4, res, *more):
+def sum_and_factor(c_ref, w_ref, r_ref, m_ref, ortho_ref, moved_ref, acc, r1, s1, r2, r4, res, *more):
     a_refs, t_refs = more[:6], more[6:12]
-    in_sem, pair_send, pair_recv, plane_send, plane_recv, line_send, line_recv = more[12:]
+    pair_send, pair_recv, plane_send, plane_recv, row_recv, line_send, line_recv = more[12:]
     wide, y = lax.axis_index("wide"), lax.axis_index("narrow")
     core, z, x = lax.rem(wide, 2), lax.rem(wide // 2, 8), wide // 16
 
@@ -153,11 +155,6 @@
 
     sibling = place(x, y, z, 1 - core)
     along_y = [place(x, lax.rem(y + d, 8), z, core) for d in range(1, 8)]
-
-    load_c = pltpu.make_async_copy(core_hbm, c_ref, in_sem.at[0])
-    load_c.start()
-    load_w = pltpu.make_async_copy(next_hbm, w_ref, in_sem.at[1])
-    load_w.start()
 
     barrier = pltpu.get_barrier_semaphore()
     for other in [sibling] + along_y:
@@ -177,42 +174,48 @@
         for b, (i, j) in enumerate(PAIRS):
             acc[k, 32*b:32*b+32] = a[128*i:128*i+128, 128*j:128*j+128].reshape(32, 4, 128)
 
+    def whole(ref, send, recv):
+        return remote(ref, ref, send, recv, sibling)
+
     def pair_out(k):
-        return remote(acc.at[k, pl.ds(96 * (1 - core), 96)], r1.at[k], pair_send.at[0, k], pair_recv.at[0, k], sibling)
-
-    def pair_back(k):
-        mine = res.at[k, pl.ds(96 * core, 96)]
-        return remote(mine, mine, pair_send.at[1, k], pair_recv.at[1, k], sibling)
-
-    def plane_out(k, d):
-        px, pz = in_plane(d)
-        return remote(s1.at[k, pl.ds(3 * (px * 8 + pz), 3)], r2.at[k, d - 1], plane_send.at[0, k, d - 1], plane_recv.at[0, k, d - 1],
-                      place(px, y, pz, core))
+        return remote(acc.at[k, pl.ds(96 * (1 - core), 96)], r1.at[k], pair_send.at[k, 4], pair_recv.at[k, 4], sibling)
 
     at = 96 * core + 3 * (x * 8 + z)
 
-    def plane_back(k, d):
-        px, pz = in_plane(d)
+    def plane_copies(make):
+        for dx in (2, 1, 3, 0):
+            def step(i, _, dx=dx):
+                dz = 1 + lax.rem(2 + i, 7) if dx == 0 else lax.rem(4 + i, 8)
+                make(dx, dz, lax.rem(x + dx, 4), lax.rem(z + dz, 8))
+                return 0
+
+            lax.fori_loop(1 if dx == 0 else 0, 8, step, 0, unroll=True)
+
+    def plane_out(k):
+        def make(dx, dz, px, pz):
+            remote(s1.at[k, pl.ds(3 * (px * 8 + pz), 3)], r2.at[k, dx * 8 + dz - 1], plane_send.at[0, k], plane_recv.at[k],
+                   place(px, y, pz, core)).start()
+
+        plane_copies(make)
+
+    def plane_back(k):
         mine = res.at[k, pl.ds(at, 3)]
-        return remote(mine, mine, plane_send.at[1, k, d - 1], plane_recv.at[1, k, d - 1], place(px, y, pz, core))
+
+        def make(dx, dz, px, pz):
+            remote(mine, mine, plane_send.at[1, k], row_recv.at[k, dx], place(px, y, pz, core)).start()
+
+        plane_copies(make)
 
     def line(k, d):
         return remote(r4.at[k, y], r4.at[k, y], line_send.at[k, d - 1], line_recv.at[k, d - 1], along_y[d - 1])
-
-    def each(what):
-        def step(d, _):
-            what(d)
-            return 0
-
-        lax.fori_loop(1, 32, step, 0)
 
     def pair_sum(k):
         pair_out(k).wait_recv()
         s1[k] = acc[k, pl.ds(96 * core, 96)] + r1[k]
-        each(lambda d: plane_out(k, d).start())
+        plane_out(k)
 
     def plane_sum(k):
-        each(lambda d: plane_out(k, d).wait_recv())
+        whole(r2.at[k], plane_send.at[0, k], plane_recv.at[k]).wait_recv()
         total = s1[k, pl.ds(3 * (x * 8 + z), 3)]
         parts = [r2[k, d] for d in range(31)]
         while len(parts) > 1:
@@ -226,18 +229,32 @@
             line(k, d).wait_recv()
         p = [r4[k, d] for d in range(8)]
         res[k, pl.ds(at, 3)] = ((p[0] + p[1]) + (p[2] + p[3])) + ((p[4] + p[5]) + (p[6] + p[7]))
-        each(lambda d: plane_back(k, d).start())
+        plane_back(k)
+
+    def pair_back(k, dx):
+        row = res.at[k, pl.ds(96 * core + 24 * lax.rem(x + 4 - dx, 4), 24)]
+        return remote(row, row, pair_send.at[k, dx], pair_recv.at[k, dx], sibling)
 
     def gathered(k):
-        each(lambda d: plane_back(k, d).wait_recv())
-        pair_back(k).start()
-
-    load_c.wait()
+        for dx in (0, 1, 3, 2):
+            rows = 21 if dx == 0 else 24
+            whole(acc.at[k, pl.ds(0, rows)], plane_send.at[1, k], row_recv.at[k, dx]).wait_recv()
+            pair_back(k, dx).start()
+
+    def sent(k):
+        pair_out(k).wait_send()
+        whole(r2.at[k], plane_send.at[0, k], plane_recv.at[k]).wait_send()
+        for d in range(1, 8):
+            line(k, d).wait_send()
+
+    def all_back(k):
+        for dx in range(4):
+            pair_back(k, dx).wait_recv()
+
     c = split(c_ref[0])
     fill(0, dot3(c, c, TN))
     pl.semaphore_wait(barrier, 39)
     pair_out(0).start()
-    load_w.wait()
     w = split(w_ref[:, 0, :])
     fill(1, dot3(w, w, NT))
     pair_out(1).start()
@@ -252,7 +269,9 @@
     line_sum(0)
     line_sum(1)
     gathered(0)
-    pair_back(0).wait_recv()
+    sent(0)
+    sent(1)
+    all_back(0)
 
     def block(k, b):
         return res[k, 32*b:32*b+32].reshape(128, 128)
@@ -282,24 +301,20 @@
         moved_ref[64*p:64*p+64, :] = dot3(rp, (w[0][o:, :], w[1][o:, :]), NN)
         if p == 1:
             gathered(1)
-    pair_back(1).wait_recv()
+    all_back(1)
     for b, (i, j) in enumerate(PAIRS):
         a = block(1, b)
         m_ref[128*i:128*i+128, 128*j:128*j+128] = a
         if i < j:
             m_ref[128*j:128*j+128, 128*i:128*i+128] = a.T
     for k in range(2):
-        pair_out(k).wait_send()
-        each(lambda d: plane_out(k, d).wait_send())
-        for d in range(1, 8):
-            line(k, d).wait_send()
-        each(lambda d: plane_back(k, d).wait_send())
-        pair_back(k).wait_send()
+        whole(r2.at[k], plane_send.at[1, k], plane_recv.at[k]).wait_send()
+        for dx in range(4):
+            pair_back(k, dx).wait_send()
 
 
 def first(core, nxt):
     v = pl.BlockSpec(memory_space=pltpu.VMEM)
-    anywhere = pl.BlockSpec(memory_space=pl.ANY)
     f32 = lambda *s: pltpu.VMEM(s, jnp.float32)
     half = lambda *lead: pltpu.VMEM(lead + (4, 128), jnp.float32)
     sems = pltpu.SemaphoreType.DMA
@@ -307,58 +322,66 @@
     return pl.pallas_call(
         sum_and_factor,
         out_shape=(square,) * 4,
-        in_specs=[anywhere] * 2, out_specs=(v,) * 4,
-        scratch_shapes=[f32(1, RANK, RANK), f32(RANK, 1, RANK), half(2, 192), half(2, 96), half(2, 96), half(2, 31, 3), half(2, 8, 3), half(2, 192)]
+        in_specs=[v] * 2, out_specs=(v,) * 4,
+        scratch_shapes=[half(2, 192), half(2, 96), half(2, 96), half(2, 31, 3), half(2, 8, 3), half(2, 192)]
         + [f32(64, RANK)] * 12
-        + [sems((2,)), sems((2, 2)), sems((2, 2)), sems((2, 2, 31)), sems((2, 2, 31)), sems((2, 7)), sems((2, 7))],
+        + [sems((2, 5)), sems((2, 5)), sems((2, 2)), sems((2,)), sems((2, 4)), sems((2, 7)), sems((2, 7))],
         compiler_params=pltpu.CompilerParams(collective_id=0, has_side_effects=True, vmem_limit_bytes=40 * 1024 * 1024),
     )(core, nxt)
 
 
-def iterate(scale, r_ref, m_ref, ortho_ref, moved_ref, s_ref, co_ref, no_ref, bh_ref, bl_ref, y_ref, p1_ref, p2_ref, f_ref):
+def iterate(scale, r_ref, m_ref, ortho_ref, moved_ref, s_ref, co_ref, no_ref, bh_ref, bl_ref, y_ref, yh_ref, yl_ref, f_ref, *p_refs):
     r = r_ref[...]
-    rm = dot6(r, m_ref[...], NN)
-    y_ref[...] = dot6(dot6(s_ref[...], rm, NN), r, NT)
-    bh_ref[...], bl_ref[...] = split(dot6(rm, r, NT))
-    p1_ref[...] = jnp.zeros_like(p1_ref)
-    p2_ref[...] = jnp.zeros_like(p2_ref)
+    rs = split(r)
+    a = jnp.concatenate([dot3(s_ref[...], rs, NN), r], axis=0)
+    a = dot3(dot3(a, m_ref[...], NN), rs, NT)
+    start = a[:192]
+    bh_ref[...], bl_ref[...] = split(a[192:])
+    y_ref[...] = jnp.zeros_like(y_ref)
+    for j in range(4):
+        y_ref[64*j:64*j+48, :] = start[48*j:48*j+48, :]
+    yh_ref[...], yl_ref[...] = split(y_ref[...])
+    for p in p_refs:
+        p[...] = jnp.zeros_like(p)
+    ph, pll = p_refs[:3], p_refs[3:]
 
     def wave(w, _):
-        y = [y_ref[64*j:64*j+64, :] for j in range(3)]
-        ys = [split(v) for v in y]
-        prev1, prev2 = p1_ref[...], p2_ref[...]
-        p1s, p2s = split(prev1), split(prev2)
+        y = [y_ref[64*j:64*j+64, :] for j in range(4)]
+        ys = [(yh_ref[64*j:64*j+64, :], yl_ref[64*j:64*j+64, :]) for j in range(4)]
+        prev = [None] + [(ph[j][...], pll[j][...]) for j in range(3)]
         stack = lambda *parts: tuple(jnp.concatenate([q[i] for q in parts], axis=0) for i in range(2))
         left = lambda q: (q[0][:, :RANK], q[1][:, :RANK])
-        e0 = dot3(ys[0], stack(ys[0], ys[1]), NT)
-        e1 = dot3(ys[1], stack(left(p1s), ys[1]), NT)
-        e2 = dot3(ys[2], stack(left(p2s), ys[2], ys[2]), NT)
-        c1, c2 = split(e1[:, :64]), split(e2[:, :128])
-        s1 = e1 - dot3(c1, stack(c1, c1), NT)
-        s2 = e2[:, 128:] - dot3(c2, stack(c2, c2), NT)
+        e = [dot3(ys[0], stack(ys[0], ys[1]), NT), dot3(ys[1], stack(left(prev[1]), ys[1]), NT),
+             dot3(ys[2], stack(left(prev[2]), ys[2], ys[3]), NT), dot3(ys[3], stack(left(prev[3]), ys[3]), NT)]
+        c = [None] + [split(e[j][:, :64*j]) for j in range(1, 4)]
+        s = [e[0]] + [e[j][:, -128:] - dot3(c[j], stack(c[j], c[j]), NT) for j in range(1, 4)]
         col = lax.broadcasted_iota(jnp.int32, (64, 128), 1)
-        g01, g2 = factor([pair(jnp.where(col < 64, e0, s1)), single(s2)], True)
-        image = dot3(stack(*ys), (bh_ref[...], bl_ref[...]), NN)
-        both = [jnp.concatenate([y[j], image[64*j:64*j+64]], axis=1) for j in range(3)]
-        x1 = both[1] - dot3(c1, p1s, NN)
-        x2 = both[2] - dot3(c2, p2s, NN)
-        n01 = dot3(inverse(g01), jnp.concatenate([both[0], x1], axis=0), NN)
-        n2 = dot3(inverse(g2), x2, NN)
-        n = [n01[:64], n01[64:], n2]
-        p2_ref[0:64, :] = prev1
-        p2_ref[64:128, :] = n[1]
-        p1_ref[...] = n[0]
-        for j in range(3):
+        groups = factor([pair(jnp.where(col < 64, s[j], s[j+1])[:48]) for j in (0, 2)], False)
+        image = dot3((yh_ref[...], yl_ref[...]), (bh_ref[...], bl_ref[...]), NN)
+        x = [jnp.concatenate([y[j], image[64*j:64*j+64]], axis=1) for j in range(4)]
+        x = [x[0]] + [x[j] - dot3(c[j], prev[j], NN) for j in range(1, 4)]
+        n = [dot3(inverse(groups[i]), jnp.concatenate(x[2*i:2*i+2], axis=0), NN) for i in range(2)]
+        n = [n[0][:64], n[0][64:], n[1][:64], n[1][64:]]
+        for j in range(4):
+            parts = split(n[j])
+            if j < 3:
+                for half, part in zip((ph, pll), parts):
+                    for k in range(2, j, -1):
+                        half[k][64*j:64*j+64, :] = half[k-1][64*j:64*j+64, :]
+                    half[j][64*j:64*j+64, :] = part
+
             @pl.when(w - j < ITERS)
             def _(j=j):
-                f_ref[64*j:64*j+64, :] = n[j][:, :RANK]
+                f_ref[48*j:48*j+48, :] = n[j][:48, :RANK]
 
             @pl.when(w >= j)
-            def _(j=j):
+            def _(j=j, parts=parts):
                 y_ref[64*j:64*j+64, :] = n[j][:, RANK:]
+                yh_ref[64*j:64*j+64, :] = parts[0][:, RANK:]
+                yl_ref[64*j:64*j+64, :] = parts[1][:, RANK:]
         return 0
 
-    lax.fori_loop(0, ITERS + 2, wave, 0)
+    lax.fori_loop(0, ITERS + 3, wave, 0)
     f = split(f_ref[...])
     co_ref[...] = scale * dot3(f, ortho_ref[...], NN)
     no_ref[:, 0, :] = dot3(f, moved_ref[...], NN)
@@ -372,7 +395,8 @@
         functools.partial(iterate, scale),
         out_shape=(jax.ShapeDtypeStruct((192, RANK), jnp.float32), jax.ShapeDtypeStruct((192, 1, RANK), jnp.float32)),
         in_specs=[v] * 5, out_specs=(v, v),
-        scratch_shapes=[bf16(RANK, RANK), bf16(RANK, RANK), f32(192, RANK), f32(64, 2 * RANK), f32(128, 2 * RANK), f32(192, RANK)],
+        scratch_shapes=[bf16(RANK, RANK), bf16(RANK, RANK), f32(256, RANK), bf16(256, RANK), bf16(256, RANK), f32(192, RANK)]
+        + [bf16(64 * j, 2 * RANK) for j in (1, 2, 3, 1, 2, 3)],
         compiler_params=pltpu.CompilerParams(vmem_limit_bytes=40 * 1024 * 1024),
     )(r, m, ortho, moved, start)
 

time: 88.6 us -> 82.7 us (0.933)
  Pallas kernels: 85.7 us -> 79.7 us
    pallas_call x1, Pallas kernels: 58.1 us -> 54.1 us  [first(): pl.pallas_call(sum_and_factor, out_shape=(square,) * 4, in_specs=[v] * 2,...]
    pallas_call x1, Pallas kernels: 27.5 us -> 25.7 us  [second(): pl.pallas_call(functools.partial(iterate, scale), out_shape=(jax.ShapeDty...]
where the time goes in v3:
time: 82.7 us; the launch traced here: 82.5 us
  Pallas kernels  79.7 us (96%)
  local copies, waits for them, and re-layouts  2.12 us (3%)
    pallas_call x1, Pallas kernels, first(): pl.pallas_call(sum_and_factor, out_shape=(square,) * 4, in_specs=[v] * 2,...  54.1 us
    pallas_call x1, Pallas kernels, second(): pl.pallas_call(functools.partial(iterate, scale), out_shape=(jax.ShapeDty...  25.7 us
    unnamed x6, local copies, waits for them, and re-layouts  2.12 us

profile of v3, /device:TPU:1, one launch (start us, length us, event | category | flops | bytes accessed | tf_op | source)
XLA Modules:
  0.0 82.5 jit_solution(4203816316889432633)
XLA Ops:
  0.6 0.0 copy-start
  0.6 1.1 %copy-done = f32[1,384,384]{2,1,0:T(8,128)S(1)} copy-done((f32[1,384,384]{2,1,0:T(8,128)S(1)}, f32[1,384,384]{2,1,0:T(8,128)}, u32[]{:S(2)}) %copy-start) | copy-done | bytes 589848
  1.7 0.0 copy-start.1
  1.7 1.1 %copy-done.1 = f32[384,1,384]{2,1,0:T(1,128)S(1)} copy-done((f32[384,1,384]{2,1,0:T(1,128)S(1)}, f32[384,1,384]{2,1,0:T(1,128)}, u32[]{:S(2)}) %copy-start.1) | copy-done | bytes 589848
  2.8 0.0 copy-start.2
  2.8 54.1 %shard_map.50 = (f32[384,384]{1,0:T(8,128)S(1)}, f32[384,384]{1,0:T(8,128)S(1)}, f32[384,384]{1,0:T(8,128)S(1)}, f32[384,384]{1,0:T(8,128)S(1)}) custom-call(f32[1,384,384]{2,1,0:T(8,128)S(1)} %copy-done, f32[384,1,384]{2,1,0:T(1,128)S(1)} %copy-done.1), custom_call_target="tpu_custom_call" | custom-call | tf_op jit(solution)/shard_map/pallas_call | solution.py:322
  56.8 0.0 copy-done.2
  56.8 25.7 %shard_map.51 = (f32[192,384]{1,0:T(8,128)}, f32[192,1,384]{2,1,0:T(1,128)}) custom-call(f32[384,384]{1,0:T(8,128)S(1)} %get-tuple-element.8.r_ref, f32[384,384]{1,0:T(8,128)S(1)} %get-tuple-element.9.m_ref, f32[384,384]{1,0:T(8,128)S(1)} %get-tuple-element.10.ortho_ref, f32[384,384]{1,0:T(8,128)S(1)} %get-tuple-element.11.moved_ref, f32[192,384]{1,0:T(8,128)S(1)} %bitcast.4), custom_call_target="tpu_custom_call" | custom-call | tf_op jit(solution)/shard_map/pallas_call | solution.py:394
Async XLA Ops:
  0.6 1.1 %copy-start = (f32[1,384,384]{2,1,0:T(8,128)S(1)}, f32[1,384,384]{2,1,0:T(8,128)}, u32[]{:S(2)}) copy-start(f32[1,384,384]{2,1,0:T(8,128)} %c_ref.1) | copy-start | bytes 1769476
  1.7 1.1 %copy-start.1 = (f32[384,1,384]{2,1,0:T(1,128)S(1)}, f32[384,1,384]{2,1,0:T(1,128)}, u32[]{:S(2)}) copy-start(f32[384,1,384]{2,1,0:T(1,128)} %w_ref.1) | copy-start | bytes 1769476
  2.8 54.1 %copy-start.2 = (f32[384,192]{0,1:T(8,128)S(1)}, f32[384,192]{0,1:T(8,128)}, u32[]{:S(2)}) copy-start(f32[384,192]{0,1:T(8,128)} %param.5) | copy-start | bytes 884740

commit v4 on v3

--- a/solution.py
+++ b/solution.py
@@ -12,14 +12,9 @@
 ITERS = 6
 MESH = pl.DeviceIdType.MESH
 PAIRS = ((0, 0), (0, 1), (0, 2), (1, 1), (1, 2), (2, 2))
-HI = lax.Precision.HIGHEST
 NN = (((1,), (0,)), ((), ()))
 NT = (((1,), (1,)), ((), ()))
 TN = (((0,), (0,)), ((), ()))
-
-
-def dot6(a, b, dims):
-    return lax.dot_general(a, b, dims, precision=HI, preferred_element_type=jnp.float32)
 
 
 def split(a):
@@ -48,8 +43,8 @@
     n = len(groups[0][1])
 
     def lanes(pair, X, t):
-        if not pair:
-            return [jnp.broadcast_to(X[:, 64+8*t+j:64+8*t+j+1], (8, 128)) for j in range(8)]
+        if pair is not True:
+            return [jnp.broadcast_to(X[:, pair+8*t+j:pair+8*t+j+1], (8, 128)) for j in range(8)]
         base = jnp.where(lane_id < 64, 0, 64)
         return [jnp.take_along_axis(X, base + (8*t + j), axis=1) for j in range(8)]
 
@@ -118,10 +113,12 @@
     return lax.broadcasted_iota(jnp.int32, (rows, 128), 0), lax.broadcasted_iota(jnp.int32, (rows, 128), 1)
 
 
-def single(s):
-    row, col = iotas(64)
-    a = jnp.where(col >= 64, s, jnp.where(col == row, 1.0, 0.0))
-    return False, [[a[8*t:8*t+8, :]] for t in range(8)]
+def rows_of_tiles(*arrays):
+    return [[a[8*t:8*t+8, :] for a in arrays] for t in range(8)]
+
+
+def joined(tiles, i):
+    return jnp.concatenate([t[i] for t in tiles], axis=0)
 
 
 def pair(s):
@@ -131,19 +128,16 @@
 
 
 def inverse(group):
-    is_pair, tiles = group
-    a = jnp.concatenate([t[-1] for t in tiles], axis=0)
-    if not is_pair:
-        return a[:, :64]
+    a = joined(group[1], 1)
     if a.shape[0] < 64:
         a = jnp.concatenate([a, jnp.zeros((64 - a.shape[0], 128), jnp.float32)], axis=0)
     row, col = iotas(128)
     return jnp.where((row < 64) == (col < 64), jnp.concatenate([a, a], axis=0), 0.0)
 
 
-def sum_and_factor(c_ref, w_ref, r_ref, m_ref, ortho_ref, moved_ref, acc, r1, s1, r2, r4, res, *more):
-    a_refs, t_refs = more[:6], more[6:12]
-    pair_send, pair_recv, plane_send, plane_recv, row_recv, line_send, line_recv = more[12:]
+def sum_and_factor(c_ref, next_hbm, r_ref, m_ref, v_ref, flat_ref, w_ref, acc, r1, s1, r2, r4, res, *more):
+    a_refs = more[:6]
+    in_sem, pair_send, pair_recv, plane_send, plane_recv, row_recv, line_send, line_recv = more[6:]
     wide, y = lax.axis_index("wide"), lax.axis_index("narrow")
     core, z, x = lax.rem(wide, 2), lax.rem(wide // 2, 8), wide // 16
 
@@ -156,6 +150,8 @@
     sibling = place(x, y, z, 1 - core)
     along_y = [place(x, lax.rem(y + d, 8), z, core) for d in range(1, 8)]
 
+    load_w = pltpu.make_async_copy(next_hbm, w_ref, in_sem)
+    load_w.start()
     barrier = pltpu.get_barrier_semaphore()
     for other in [sibling] + along_y:
         pl.semaphore_signal(barrier, inc=1, device_id=other, device_id_type=MESH)
@@ -255,13 +251,14 @@
     fill(0, dot3(c, c, TN))
     pl.semaphore_wait(barrier, 39)
     pair_out(0).start()
-    w = split(w_ref[:, 0, :])
+    pair_sum(0)
+    load_w.wait()
+    w = w_ref[:, 0, :]
+    flat_ref[...] = w
+    w = split(w)
     fill(1, dot3(w, w, NT))
     pair_out(1).start()
-    pair_sum(0)
-    turned = c_ref[0].T
-    for q in range(6):
-        t_refs[q][...] = turned[64*q:64*q+64, :]
+    v_ref[...] = jnp.zeros_like(v_ref)
     r_ref[...] = jnp.zeros_like(r_ref)
     pair_sum(1)
     plane_sum(0)
@@ -280,25 +277,50 @@
         a = block(0, b)
         a_refs[2*i][:, 128*j:128*j+128] = a[:64]
         a_refs[2*i+1][:, 128*j:128*j+128] = a[64:]
+    row, col = iotas(64)
+    eye = jnp.where(col == row, 1.0, 0.0)
     for p in range(6):
         o = 128 * (p // 2)
-        d = a_refs[p][:, o:o+128]
+        here = a_refs[p][:, o:o+128]
         if p % 2 == 0:
-            d = pltpu.roll(d, 64, 1)
-        (g,) = factor([single(d)], False)
-        li = inverse(g)
-        rp = dot6(li, a_refs[p][:, o:], NN)
-        if p % 2:
-            rp = jnp.where(lax.broadcasted_iota(jnp.int32, rp.shape, 1) >= 64, rp, 0.0)
-        r_ref[64*p:64*p+64, o:] = rp
-        ortho = dot3(li, t_refs[p][...], NN)
-        ortho_ref[64*p:64*p+64, :] = ortho
+            ((_, tiles),) = factor([(0, rows_of_tiles(here, eye))], False)
+            own = joined(tiles, 1)
+            li = own[:, :64]
+            near = joined(tiles, 0)
+            near = jnp.where((col >= 64) | (col >= row), near, 0.0)
+            r_ref[64*p:64*p+64, o:o+128] = near
+            rp = near
+            a_refs[p+1][:, o:o+128] -= dot3(near[:, 64:], near, TN)
+            far = o + 128
+        else:
+            more_tiles = [a_refs[p][:, o+128:o+256]] if p < 5 else []
+            ((_, tiles),) = factor([(64, rows_of_tiles(jnp.where(col >= 64, here, eye), *more_tiles))], False)
+            first_tile = joined(tiles, 0)
+            li = first_tile[:, :64]
+            own = pltpu.roll(jnp.where(col < 64, first_tile, 0.0), 64, 1)
+            r_ref[64*p:64*p+64, o:o+128] = jnp.where(col - 64 >= row, first_tile, 0.0)
+            rp = jnp.where(col - 64 >= row, first_tile, 0.0)
+            if p < 5:
+                near = joined(tiles, 1)
+                r_ref[64*p:64*p+64, o+128:o+256] = near
+                rp = jnp.concatenate([rp, near], axis=1)
+                a_refs[p+1][:, o+128:o+256] -= dot3(near[:, :64], near, TN)
+            far = o + 256
+        if far < RANK:
+            rest = dot3(li, a_refs[p][:, far:], NN)
+            r_ref[64*p:64*p+64, far:] = rest
+            rp = jnp.concatenate([rp, rest], axis=1)
         for q in range(p + 1, 6):
             oq = 128 * (q // 2)
             lq = rp[:, 64*q-o:64*q-o+64]
-            a_refs[q][:, oq:] -= dot6(lq, rp[:, oq-o:], TN)
-            t_refs[q][...] -= dot3(lq, ortho, TN)
-        moved_ref[64*p:64*p+64, :] = dot3(rp, (w[0][o:, :], w[1][o:, :]), NN)
+            if q == p + 1:
+                oq += 128
+            if oq < RANK:
+                a_refs[q][:, oq:] -= dot3(lq, rp[:, oq-o:], TN)
+        if p:
+            earlier = dot3(r_ref[:64*p, 64*p:64*p+64], v_ref[:64*p, :o+128], TN)
+            v_ref[64*p:64*p+64, :o+128] = -dot3(li, earlier, NN)
+        v_ref[64*p:64*p+64, o:o+128] += own
         if p == 1:
             gathered(1)
     all_back(1)
@@ -322,15 +344,15 @@
     return pl.pallas_call(
         sum_and_factor,
         out_shape=(square,) * 4,
-        in_specs=[v] * 2, out_specs=(v,) * 4,
-        scratch_shapes=[half(2, 192), half(2, 96), half(2, 96), half(2, 31, 3), half(2, 8, 3), half(2, 192)]
-        + [f32(64, RANK)] * 12
-        + [sems((2, 5)), sems((2, 5)), sems((2, 2)), sems((2,)), sems((2, 4)), sems((2, 7)), sems((2, 7))],
-        compiler_params=pltpu.CompilerParams(collective_id=0, has_side_effects=True, vmem_limit_bytes=40 * 1024 * 1024),
+        in_specs=[v, pl.BlockSpec(memory_space=pl.ANY)], out_specs=(v,) * 4,
+        scratch_shapes=[f32(RANK, 1, RANK), half(2, 192), half(2, 96), half(2, 96), half(2, 31, 3), half(2, 8, 3), half(2, 192)]
+        + [f32(64, RANK)] * 6
+        + [sems(()), sems((2, 5)), sems((2, 5)), sems((2, 2)), sems((2,)), sems((2, 4)), sems((2, 7)), sems((2, 7))],
+        compiler_params=pltpu.CompilerParams(collective_id=0, has_side_effects=True, vmem_limit_bytes=51 * 1024 * 1024),
     )(core, nxt)
 
 
-def iterate(scale, r_ref, m_ref, ortho_ref, moved_ref, s_ref, co_ref, no_ref, bh_ref, bl_ref, y_ref, yh_ref, yl_ref, f_ref, *p_refs):
+def iterate(scale, r_ref, m_ref, v_ref, w_ref, s_ref, c_ref, co_ref, no_ref, bh_ref, bl_ref, y_ref, yh_ref, yl_ref, f_ref, *p_refs):
     r = r_ref[...]
     rs = split(r)
     a = jnp.concatenate([dot3(s_ref[...], rs, NN), r], axis=0)
@@ -383,28 +405,28 @@
 
     lax.fori_loop(0, ITERS + 3, wave, 0)
     f = split(f_ref[...])
-    co_ref[...] = scale * dot3(f, ortho_ref[...], NN)
-    no_ref[:, 0, :] = dot3(f, moved_ref[...], NN)
-
-
-def second(r, m, ortho, moved, start, scale):
-    v = pl.BlockSpec(memory_space=pltpu.VMEM)
+    co_ref[...] = scale * dot3(dot3(f, v_ref[...], NN), c_ref[0], NT)
+    no_ref[:, 0, :] = dot3(dot3(f, r_ref[...], NN), w_ref[...], NN)
+
+
+def second(r, m, v, w, start, core, scale):
+    vmem = pl.BlockSpec(memory_space=pltpu.VMEM)
     f32 = lambda *s: pltpu.VMEM(s, jnp.float32)
     bf16 = lambda *s: pltpu.VMEM(s, jnp.bfloat16)
     return pl.pallas_call(
         functools.partial(iterate, scale),
         out_shape=(jax.ShapeDtypeStruct((192, RANK), jnp.float32), jax.ShapeDtypeStruct((192, 1, RANK), jnp.float32)),
-        in_specs=[v] * 5, out_specs=(v, v),
+        in_specs=[vmem] * 6, out_specs=(vmem, vmem),
         scratch_shapes=[bf16(RANK, RANK), bf16(RANK, RANK), f32(256, RANK), bf16(256, RANK), bf16(256, RANK), f32(192, RANK)]
         + [bf16(64 * j, 2 * RANK) for j in (1, 2, 3, 1, 2, 3)],
         compiler_params=pltpu.CompilerParams(vmem_limit_bytes=40 * 1024 * 1024),
-    )(r, m, ortho, moved, start)
+    )(r, m, v, w, start, core)
 
 
 def shards(core, next_core, start_block):
-    r, m, ortho, moved = first(core, next_core)
+    r, m, v, w = first(core, next_core)
     scale = math.sqrt(core.shape[0] * lax.axis_size("wide") * lax.axis_size("narrow") * core.shape[1])
-    core_t, next_out = second(r, m, ortho, moved, start_block.T, scale)
+    core_t, next_out = second(r, m, v, w, start_block.T, core, scale)
     return core_t.T[None], next_out
 
 

time: 82.7 us -> 77.6 us (0.938)
  Pallas kernels: 79.7 us -> 75.8 us
  local copies, waits for them, and re-layouts: 2.12 us -> 1.06 us
    pallas_call x1, Pallas kernels: 54.1 us -> 49.1 us  [first(): pl.pallas_call(sum_and_factor, out_shape=(square,) * 4, in_specs=[v, pl.B...]
    unnamed x6 -> x4, local copies, waits for them, and re-layouts: 2.12 us -> 1.06 us
    pallas_call x1, Pallas kernels: 25.7 us -> 26.6 us  [second(): pl.pallas_call(functools.partial(iterate, scale), out_shape=(jax.ShapeDty...]
where the time goes in v4:
time: 77.6 us; the launch traced here: 77.5 us
  Pallas kernels  75.8 us (98%)
  local copies, waits for them, and re-layouts  1.06 us (1%)
    pallas_call x1, Pallas kernels, first(): pl.pallas_call(sum_and_factor, out_shape=(square,) * 4, in_specs=[v, pl.B...  49.1 us
    pallas_call x1, Pallas kernels, second(): pl.pallas_call(functools.partial(iterate, scale), out_shape=(jax.ShapeDty...  26.6 us

profile of v4, /device:TPU:1, one launch (start us, length us, event | category | flops | bytes accessed | tf_op | source)
XLA Modules:
  0.0 77.5 jit_solution(12899126259465753840)
XLA Ops:
  0.6 0.0 copy-start
  0.6 1.1 %copy-done = f32[1,384,384]{2,1,0:T(8,128)S(1)} copy-done((f32[1,384,384]{2,1,0:T(8,128)S(1)}, f32[1,384,384]{2,1,0:T(8,128)}, u32[]{:S(2)}) %copy-start) | copy-done | bytes 589848
  1.7 0.0 copy-start.1
  1.7 49.1 %shard_map.50 = (f32[384,384]{1,0:T(8,128)S(1)}, f32[384,384]{1,0:T(8,128)S(1)}, f32[384,384]{1,0:T(8,128)S(1)}, f32[384,384]{1,0:T(8,128)S(1)}) custom-call(f32[1,384,384]{2,1,0:T(8,128)S(1)} %copy-done, f32[384,1,384]{2,1,0:T(1,128)} %next_hbm.1), custom_call_target="tpu_custom_call" | custom-call | tf_op jit(solution)/shard_map/pallas_call | solution.py:344
  50.8 0.0 copy-done.1
  50.8 26.6 %shard_map.51 = (f32[192,384]{1,0:T(8,128)}, f32[192,1,384]{2,1,0:T(1,128)}) custom-call(f32[384,384]{1,0:T(8,128)S(1)} %get-tuple-element.8.r_ref, f32[384,384]{1,0:T(8,128)S(1)} %get-tuple-element.9.m_ref, f32[384,384]{1,0:T(8,128)S(1)} %get-tuple-element.10.v_ref, f32[384,384]{1,0:T(8,128)S(1)} %get-tuple-element.11.w_ref, f32[192,384]{1,0:T(8,128)S(1)} %bitcast.4, ...), custom_call_target="tpu_custom_call" | custom-call | tf_op jit(solution)/shard_map/pallas_call | solution.py:416
Async XLA Ops:
  0.6 1.1 %copy-start = (f32[1,384,384]{2,1,0:T(8,128)S(1)}, f32[1,384,384]{2,1,0:T(8,128)}, u32[]{:S(2)}) copy-start(f32[1,384,384]{2,1,0:T(8,128)} %c_ref.3) | copy-start | bytes 1769476
  1.7 49.1 %copy-start.1 = (f32[384,192]{0,1:T(8,128)S(1)}, f32[384,192]{0,1:T(8,128)}, u32[]{:S(2)}) copy-start(f32[384,192]{0,1:T(8,128)} %param.5) | copy-start | bytes 884740

commit v5 on v4

--- a/solution.py
+++ b/solution.py
@@ -63,12 +63,14 @@
             others = range(t+2, n)
             if not gj:
                 co = {u: lanes(pair, A[u][0], t) for u in others}
+            dj = row_of(cb[0], 0)
             for j in range(8):
-                dj = row_of(cb[j], j)
                 r = 1.0 / dj
                 dv = dj if j == 0 else jnp.where(sub == j, dj, dv)
                 rows = [row_of(p, j) for p in P]
                 bs = {i: row_of(cb[j], i) for i in range(j+1, 8)}
+                if j < 7:
+                    dj = row_of(cb[j+1], j+1) - (bs[j+1] * bs[j+1]) * r
                 if gj:
                     rv = r if j == 0 else jnp.where(sub == j, r, rv)
                     mg = jnp.where(sub == j, 0.0, cb[j] * r)
@@ -135,7 +137,7 @@
     return jnp.where((row < 64) == (col < 64), jnp.concatenate([a, a], axis=0), 0.0)
 
 
-def sum_and_factor(c_ref, next_hbm, r_ref, m_ref, v_ref, flat_ref, w_ref, acc, r1, s1, r2, r4, res, *more):
+def sum_and_factor(c_ref, next_hbm, r_ref, rm_ref, v_ref, flat_ref, w_ref, m_ref, acc, r1, s1, r2, r4, res, *more):
     a_refs = more[:6]
     in_sem, pair_send, pair_recv, plane_send, plane_recv, row_recv, line_send, line_recv = more[6:]
     wide, y = lax.axis_index("wide"), lax.axis_index("narrow")
@@ -323,12 +325,16 @@
         v_ref[64*p:64*p+64, o:o+128] += own
         if p == 1:
             gathered(1)
-    all_back(1)
-    for b, (i, j) in enumerate(PAIRS):
-        a = block(1, b)
-        m_ref[128*i:128*i+128, 128*j:128*j+128] = a
-        if i < j:
-            m_ref[128*j:128*j+128, 128*i:128*i+128] = a.T
+        if p == 3:
+            all_back(1)
+            for b, (i, j) in enumerate(PAIRS):
+                a = block(1, b)
+                m_ref[128*i:128*i+128, 128*j:128*j+128] = a
+                if i < j:
+                    m_ref[128*j:128*j+128, 128*i:128*i+128] = a.T
+            rm_ref[:256, :] = dot3(r_ref[:256, :], m_ref[...], NN)
+        if p > 3:
+            rm_ref[64*p:64*p+64, :] = dot3(rp, m_ref[o:, :], NN)
     for k in range(2):
         whole(r2.at[k], plane_send.at[1, k], plane_recv.at[k]).wait_send()
         for dx in range(4):
@@ -345,88 +351,86 @@
         sum_and_factor,
         out_shape=(square,) * 4,
         in_specs=[v, pl.BlockSpec(memory_space=pl.ANY)], out_specs=(v,) * 4,
-        scratch_shapes=[f32(RANK, 1, RANK), half(2, 192), half(2, 96), half(2, 96), half(2, 31, 3), half(2, 8, 3), half(2, 192)]
+        scratch_shapes=[f32(RANK, 1, RANK), f32(RANK, RANK), half(2, 192), half(2, 96), half(2, 96), half(2, 31, 3), half(2, 8, 3), half(2, 192)]
         + [f32(64, RANK)] * 6
         + [sems(()), sems((2, 5)), sems((2, 5)), sems((2, 2)), sems((2,)), sems((2, 4)), sems((2, 7)), sems((2, 7))],
         compiler_params=pltpu.CompilerParams(collective_id=0, has_side_effects=True, vmem_limit_bytes=51 * 1024 * 1024),
     )(core, nxt)
 
 
-def iterate(scale, r_ref, m_ref, v_ref, w_ref, s_ref, c_ref, co_ref, no_ref, bh_ref, bl_ref, y_ref, yh_ref, yl_ref, f_ref, *p_refs):
-    r = r_ref[...]
-    rs = split(r)
-    a = jnp.concatenate([dot3(s_ref[...], rs, NN), r], axis=0)
-    a = dot3(dot3(a, m_ref[...], NN), rs, NT)
-    start = a[:192]
-    bh_ref[...], bl_ref[...] = split(a[192:])
-    y_ref[...] = jnp.zeros_like(y_ref)
-    for j in range(4):
-        y_ref[64*j:64*j+48, :] = start[48*j:48*j+48, :]
-    yh_ref[...], yl_ref[...] = split(y_ref[...])
-    for p in p_refs:
-        p[...] = jnp.zeros_like(p)
-    ph, pll = p_refs[:3], p_refs[3:]
-
-    def wave(w, _):
-        y = [y_ref[64*j:64*j+64, :] for j in range(4)]
-        ys = [(yh_ref[64*j:64*j+64, :], yl_ref[64*j:64*j+64, :]) for j in range(4)]
-        prev = [None] + [(ph[j][...], pll[j][...]) for j in range(3)]
-        stack = lambda *parts: tuple(jnp.concatenate([q[i] for q in parts], axis=0) for i in range(2))
-        left = lambda q: (q[0][:, :RANK], q[1][:, :RANK])
-        e = [dot3(ys[0], stack(ys[0], ys[1]), NT), dot3(ys[1], stack(left(prev[1]), ys[1]), NT),
-             dot3(ys[2], stack(left(prev[2]), ys[2], ys[3]), NT), dot3(ys[3], stack(left(prev[3]), ys[3]), NT)]
-        c = [None] + [split(e[j][:, :64*j]) for j in range(1, 4)]
-        s = [e[0]] + [e[j][:, -128:] - dot3(c[j], stack(c[j], c[j]), NT) for j in range(1, 4)]
-        col = lax.broadcasted_iota(jnp.int32, (64, 128), 1)
-        groups = factor([pair(jnp.where(col < 64, s[j], s[j+1])[:48]) for j in (0, 2)], False)
-        image = dot3((yh_ref[...], yl_ref[...]), (bh_ref[...], bl_ref[...]), NN)
-        x = [jnp.concatenate([y[j], image[64*j:64*j+64]], axis=1) for j in range(4)]
-        x = [x[0]] + [x[j] - dot3(c[j], prev[j], NN) for j in range(1, 4)]
-        n = [dot3(inverse(groups[i]), jnp.concatenate(x[2*i:2*i+2], axis=0), NN) for i in range(2)]
-        n = [n[0][:64], n[0][64:], n[1][:64], n[1][64:]]
-        for j in range(4):
-            parts = split(n[j])
-            if j < 3:
-                for half, part in zip((ph, pll), parts):
-                    for k in range(2, j, -1):
-                        half[k][64*j:64*j+64, :] = half[k-1][64*j:64*j+64, :]
-                    half[j][64*j:64*j+64, :] = part
-
-            @pl.when(w - j < ITERS)
-            def _(j=j):
-                f_ref[48*j:48*j+48, :] = n[j][:48, :RANK]
-
-            @pl.when(w >= j)
-            def _(j=j, parts=parts):
-                y_ref[64*j:64*j+64, :] = n[j][:, RANK:]
-                yh_ref[64*j:64*j+64, :] = parts[0][:, RANK:]
-                yl_ref[64*j:64*j+64, :] = parts[1][:, RANK:]
-        return 0
-
-    lax.fori_loop(0, ITERS + 3, wave, 0)
-    f = split(f_ref[...])
+def iterate(scale, r_ref, rm_ref, v_ref, w_ref, s_ref, c_ref, co_ref, no_ref):
+    rm = rm_ref[...]
+    a = dot3(jnp.concatenate([dot3(s_ref[...], rm, NN), rm], axis=0), r_ref[...], NT)
+    bond = split(a[192:])
+    pad = jnp.zeros((16, RANK), jnp.float32)
+    stack = lambda *parts: tuple(jnp.concatenate([q[i] for q in parts], axis=0) for i in range(2))
+    left = lambda q: (q[0][:, :RANK], q[1][:, :RANK])
+    row, col = iotas(64)
+    eyes = jnp.where((col == row) | (col == row + 64), 1.0, 0.0)
+    y = [jnp.concatenate([a[48*j:48*j+48], pad], axis=0) for j in range(4)]
+    ys = [split(v) for v in y]
+    done, basis = {}, [None] * 4
+    for w in range(ITERS + 3):
+        turn = {j: w - j for j in range(4) if 0 <= w - j < ITERS}
+        prev, c, s = {}, {}, {}
+        for j, k in turn.items():
+            if j == 0:
+                s[j] = dot3(ys[j], stack(ys[j], ys[j]), NT)
+                continue
+            prev[j] = stack(*[done[i, k] for i in range(j)])
+            e = dot3(ys[j], stack(left(prev[j]), ys[j], *([ys[j]] if j == 2 else [])), NT)
+            c[j] = split(e[:, :64*j])
+            s[j] = e[:, -128:] - dot3(c[j], stack(c[j], c[j]), NT)
+        pairs = [i for i in (0, 2) if i in turn or i + 1 in turn]
+        groups = factor([pair(jnp.where(col < 64, s.get(i, eyes), s.get(i + 1, eyes))[:48]) for i in pairs], False)
+        onward = [j for j, k in turn.items() if k < ITERS - 1]
+        image = dot3(stack(*[ys[j] for j in onward]), bond, NN) if onward else None
+        for i, group in zip(pairs, groups):
+            wide = any(j in onward for j in (i, i + 1))
+            xs = []
+            for j in (i, i + 1):
+                if j in onward:
+                    at = 64 * onward.index(j)
+                    x = jnp.concatenate([y[j], image[at:at+64]], axis=1)
+                elif j in turn:
+                    x = y[j]
+                else:
+                    x = jnp.zeros((64, 2 * RANK if wide else RANK), jnp.float32)
+                if j in prev:
+                    x = x - dot3(c[j], prev[j] if j in onward else left(prev[j]), NN)
+                if wide and x.shape[1] == RANK:
+                    x = jnp.concatenate([x, jnp.zeros((64, RANK), jnp.float32)], axis=1)
+                xs.append(x)
+            n = dot3(inverse(group), jnp.concatenate(xs, axis=0), NN)
+            for j in (i, i + 1):
+                if j not in turn:
+                    continue
+                own = n[64*(j-i):64*(j-i)+64]
+                done[j, turn[j]] = split(own if j in onward else own[:, :RANK])
+                if j in onward:
+                    y[j] = own[:, RANK:]
+                    ys[j] = tuple(q[:, RANK:] for q in done[j, turn[j]])
+                else:
+                    basis[j] = own[:48, :RANK]
+    f = split(jnp.concatenate(basis, axis=0))
     co_ref[...] = scale * dot3(dot3(f, v_ref[...], NN), c_ref[0], NT)
     no_ref[:, 0, :] = dot3(dot3(f, r_ref[...], NN), w_ref[...], NN)
 
 
-def second(r, m, v, w, start, core, scale):
+def second(r, rm, v, w, start, core, scale):
     vmem = pl.BlockSpec(memory_space=pltpu.VMEM)
-    f32 = lambda *s: pltpu.VMEM(s, jnp.float32)
-    bf16 = lambda *s: pltpu.VMEM(s, jnp.bfloat16)
     return pl.pallas_call(
         functools.partial(iterate, scale),
         out_shape=(jax.ShapeDtypeStruct((192, RANK), jnp.float32), jax.ShapeDtypeStruct((192, 1, RANK), jnp.float32)),
         in_specs=[vmem] * 6, out_specs=(vmem, vmem),
-        scratch_shapes=[bf16(RANK, RANK), bf16(RANK, RANK), f32(256, RANK), bf16(256, RANK), bf16(256, RANK), f32(192, RANK)]
-        + [bf16(64 * j, 2 * RANK) for j in (1, 2, 3, 1, 2, 3)],
         compiler_params=pltpu.CompilerParams(vmem_limit_bytes=40 * 1024 * 1024),
-    )(r, m, v, w, start, core)
+    )(r, rm, v, w, start, core)
 
 
 def shards(core, next_core, start_block):
-    r, m, v, w = first(core, next_core)
+    r, rm, v, w = first(core, next_core)
     scale = math.sqrt(core.shape[0] * lax.axis_size("wide") * lax.axis_size("narrow") * core.shape[1])
-    core_t, next_out = second(r, m, v, w, start_block.T, core, scale)
+    core_t, next_out = second(r, rm, v, w, start_block.T, core, scale)
     return core_t.T[None], next_out
 
 

time: 77.6 us -> 71.9 us (0.927)
  Pallas kernels: 75.8 us -> 70 us
    pallas_call x1, Pallas kernels: 26.6 us -> 20.9 us  [second(): pl.pallas_call(functools.partial(iterate, scale), out_shape=(jax.ShapeDty...]
where the time goes in v5:
time: 71.9 us; the launch traced here: 71.7 us
  Pallas kernels  70 us (97%)
  local copies, waits for them, and re-layouts  1.06 us (1%)
    pallas_call x1, Pallas kernels, first(): pl.pallas_call(sum_and_factor, out_shape=(square,) * 4, in_specs=[v, pl.B...  49.1 us
    pallas_call x1, Pallas kernels, second(): pl.pallas_call(functools.partial(iterate, scale), out_shape=(jax.ShapeDty...  20.9 us

profile of v5, /device:TPU:1, one launch (start us, length us, event | category | flops | bytes accessed | tf_op | source)
XLA Modules:
  0.0 71.7 jit_solution(9197577757935196008)
XLA Ops:
  0.6 0.0 copy-start
  0.6 1.1 %copy-done = f32[1,384,384]{2,1,0:T(8,128)S(1)} copy-done((f32[1,384,384]{2,1,0:T(8,128)S(1)}, f32[1,384,384]{2,1,0:T(8,128)}, u32[]{:S(2)}) %copy-start) | copy-done | bytes 589848
  1.7 0.0 copy-start.1
  1.7 49.1 %shard_map.50 = (f32[384,384]{1,0:T(8,128)S(1)}, f32[384,384]{1,0:T(8,128)S(1)}, f32[384,384]{1,0:T(8,128)S(1)}, f32[384,384]{1,0:T(8,128)S(1)}) custom-call(f32[1,384,384]{2,1,0:T(8,128)S(1)} %copy-done, f32[384,1,384]{2,1,0:T(1,128)} %next_hbm.1), custom_call_target="tpu_custom_call" | custom-call | tf_op jit(solution)/shard_map/pallas_call | solution.py:350
  50.8 0.0 copy-done.1
  50.8 20.9 %shard_map.51 = (f32[192,384]{1,0:T(8,128)}, f32[192,1,384]{2,1,0:T(1,128)}) custom-call(f32[384,384]{1,0:T(8,128)S(1)} %get-tuple-element.8.r_ref, f32[384,384]{1,0:T(8,128)S(1)} %get-tuple-element.9.rm_ref, f32[384,384]{1,0:T(8,128)S(1)} %get-tuple-element.10.v_ref, f32[384,384]{1,0:T(8,128)S(1)} %get-tuple-element.11.w_ref, f32[192,384]{1,0:T(8,128)S(1)} %bitcast.4, ...), custom_call_target="tpu_custom_call" | custom-call | tf_op jit(solution)/shard_map/pallas_call | solution.py:422
Async XLA Ops:
  0.6 1.1 %copy-start = (f32[1,384,384]{2,1,0:T(8,128)S(1)}, f32[1,384,384]{2,1,0:T(8,128)}, u32[]{:S(2)}) copy-start(f32[1,384,384]{2,1,0:T(8,128)} %c_ref.3) | copy-start | bytes 1769476
  1.7 49.1 %copy-start.1 = (f32[384,192]{0,1:T(8,128)S(1)}, f32[384,192]{0,1:T(8,128)}, u32[]{:S(2)}) copy-start(f32[384,192]{0,1:T(8,128)} %param.5) | copy-start | bytes 884740

commit v6 on v5

--- a/solution.py
+++ b/solution.py
@@ -249,10 +249,22 @@
         for dx in range(4):
             pair_back(k, dx).wait_recv()
 
-    c = split(c_ref[0])
-    fill(0, dot3(c, c, TN))
+    def gram_part(h):
+        c = split(c_ref[0])
+        wide = slice(128 * h, RANK)
+        rows = slice(0, 128) if h == 0 else wide
+        a = dot3(tuple(q[:, rows] for q in c), tuple(q[:, wide] for q in c), TN)
+        for b, (i, j) in enumerate(PAIRS):
+            if (i > 0) == (h > 0):
+                i, j = i - h, j - h
+                acc[0, 32*b:32*b+32] = a[128*i:128*i+128, 128*j:128*j+128].reshape(32, 4, 128)
+
+    pl.when(core == 1)(lambda: gram_part(0))
+    pl.when(core == 0)(lambda: gram_part(1))
     pl.semaphore_wait(barrier, 39)
     pair_out(0).start()
+    pl.when(core == 1)(lambda: gram_part(1))
+    pl.when(core == 0)(lambda: gram_part(0))
     pair_sum(0)
     load_w.wait()
     w = w_ref[:, 0, :]

time: 71.9 us -> 71.8 us (level)
  no operation moved by 1% of the time
where the time goes in v6:
time: 71.8 us; the launch traced here: 71.7 us
  Pallas kernels  70 us (97%)
  local copies, waits for them, and re-layouts  1.06 us (1%)
    pallas_call x1, Pallas kernels, first(): pl.pallas_call(sum_and_factor, out_shape=(square,) * 4, in_specs=[v, pl.B...  49.1 us
    pallas_call x1, Pallas kernels, second(): pl.pallas_call(functools.partial(iterate, scale), out_shape=(jax.ShapeDty...  20.9 us

profile of v6, /device:TPU:1, one launch (start us, length us, event | category | flops | bytes accessed | tf_op | source)
XLA Modules:
  0.0 71.7 jit_solution(9068349533704768787)
XLA Ops:
  0.6 0.0 copy-start
  0.6 1.1 %copy-done = f32[1,384,384]{2,1,0:T(8,128)S(1)} copy-done((f32[1,384,384]{2,1,0:T(8,128)S(1)}, f32[1,384,384]{2,1,0:T(8,128)}, u32[]{:S(2)}) %copy-start) | copy-done | bytes 589848
  1.7 0.0 copy-start.1
  1.7 49.1 %shard_map.50 = (f32[384,384]{1,0:T(8,128)S(1)}, f32[384,384]{1,0:T(8,128)S(1)}, f32[384,384]{1,0:T(8,128)S(1)}, f32[384,384]{1,0:T(8,128)S(1)}) custom-call(f32[1,384,384]{2,1,0:T(8,128)S(1)} %copy-done, f32[384,1,384]{2,1,0:T(1,128)} %next_hbm.1), custom_call_target="tpu_custom_call" | custom-call | tf_op jit(solution)/shard_map/pallas_call | solution.py:362
  50.8 0.0 copy-done.1
  50.8 20.9 %shard_map.51 = (f32[192,384]{1,0:T(8,128)}, f32[192,1,384]{2,1,0:T(1,128)}) custom-call(f32[384,384]{1,0:T(8,128)S(1)} %get-tuple-element.8.r_ref, f32[384,384]{1,0:T(8,128)S(1)} %get-tuple-element.9.rm_ref, f32[384,384]{1,0:T(8,128)S(1)} %get-tuple-element.10.v_ref, f32[384,384]{1,0:T(8,128)S(1)} %get-tuple-element.11.w_ref, f32[192,384]{1,0:T(8,128)S(1)} %bitcast.4, ...), custom_call_target="tpu_custom_call" | custom-call | tf_op jit(solution)/shard_map/pallas_call | solution.py:434
Async XLA Ops:
  0.6 1.1 %copy-start = (f32[1,384,384]{2,1,0:T(8,128)S(1)}, f32[1,384,384]{2,1,0:T(8,128)}, u32[]{:S(2)}) copy-start(f32[1,384,384]{2,1,0:T(8,128)} %c_ref.3) | copy-start | bytes 1769476
  1.7 49.1 %copy-start.1 = (f32[384,192]{0,1:T(8,128)S(1)}, f32[384,192]{0,1:T(8,128)}, u32[]{:S(2)}) copy-start(f32[384,192]{0,1:T(8,128)} %param.5) | copy-start | bytes 884740
